TPU v7x, 128 devices: a whole 4x4x4 slice. The times are simulated.
128 devices in a mesh: fx: 16 (over y, z), fy: 8 (over x, core).
Axes of the slice: x: 4, y: 4, z: 4, core: 2. Of those that a mesh axis runs over, the one named last changes fastest.
Arguments:
- state: float32 [256, 48, 2048], P('fy', None, 'fx'), may hold values from -6 to 6
- coef: float32 [256, 2048], P('fy', 'fx'), may hold values from 0.05 to 0.24
- weight_table: float32 [64, 128, 128], replicated, may hold values from -0.5 to 0.5
- src_blocks: int32 [128, 128, 4], P(('fx', 'fy')), may hold values from 0 to 31
- dst_blocks: int32 [128, 128, 4], P(('fx', 'fy')), may hold values from 0 to 31
- weight_rows: int32 [128, 128, 4], P(('fx', 'fy')), may hold values from 0 to 63
- counts: int32 [128, 128], P(('fx', 'fy')), may hold values from 1 to 4, as said below
- brackets: int32 [13], replicated, may hold values from 0 to 14
- fractions: float32 [13], replicated, may hold values from 0 to 1
- w_in: bfloat16 [512, 39], replicated, may hold values from -1 to 1
- b_in: float32 [512], replicated, may hold values from -4 to 4
- w_mid: bfloat16 [512, 512], replicated, may hold values from -0.25 to 0.25
- b_mid: float32 [512], replicated, may hold values from -4 to 4
- w_out: bfloat16 [39, 512], replicated, may hold values from -0.25 to 0.25
Outputs:
- diffused_state: float32 [256, 48, 2048], P('fy', None, 'fx')
- tendency: float32 [256, 48, 2048], P('fy', None, 'fx')
Inputs may be any that keep to these rules, and one draw needn't show every extreme that they name: At most 4 slots are used from one device to one owner; in every draw one owner receives 4 from every device. Slots at positions counts and beyond hold padding in src_blocks, dst_blocks and weight_rows.
All inputs are finite; a program needn't handle non-finite values.
Results may differ from a plain program's by a relative error of at most 0.0037.
Values sent between devices are 32-bit elements; how exact they have to be, the bound alone decides.
No kernel may reach another device: no remote copies, remote signals or barrier semaphores. Data moves between devices by JAX's collectives and lax.ppermute only.
A program may use at most 128 MiB of HBM per device.

v0:
```python
import jax
import jax.numpy as jnp
from jax import lax
from jax.sharding import PartitionSpec as P

LEV = 16
SWEEPS = 4


HIGH_ACCURACY = lax.Precision.HIGHEST


def padded(block, sides, width, periodic):
    for axis, dim in sides:
        count = lax.axis_size(axis)
        forward = [(i, i + 1) for i in range(count - 1)]
        if periodic:
            forward.append((count - 1, 0))
        backward = [(target, source) for source, target in forward]
        low = lax.ppermute(
            lax.slice_in_dim(block, block.shape[dim] - width, None, axis=dim), axis, forward
        )
        high = lax.ppermute(lax.slice_in_dim(block, 0, width, axis=dim), axis, backward)
        block = jnp.concatenate([low, block, high], axis=dim)
    return block


def level_matrix(brackets, fractions, levels):
    cols = jnp.arange(levels, dtype=jnp.int32)
    lower = (cols[None, :] == brackets[:, None]).astype(jnp.float32)
    upper = (cols[None, :] == brackets[:, None] + 1).astype(jnp.float32)
    return lower * (1.0 - fractions[:, None]) + upper * fractions[:, None]


def apply_levels(values, remap_matrix):
    levels = remap_matrix.shape[1]
    lead = values.shape[:-2]
    width = values.shape[-1]
    divided_parts = values.reshape(lead + (values.shape[-2] // levels, levels, width))
    relocated_rows = jnp.einsum(
        "fm,...qme->...qfe", remap_matrix, divided_parts, precision=HIGH_ACCURACY
    )
    return relocated_rows.reshape(lead + (-1, width))


def remap_blocks(rows, indices, table, transpose):
    total = rows.shape[0]
    group = min(64, total)
    rows_grouped = rows.reshape((total // group, group) + rows.shape[1:])
    index_grouped = indices.reshape(total // group, group)

    def one_group(pair):
        part, index = pair
        remap_matrices = jnp.take(table, index, axis=0)
        if transpose:
            return jnp.einsum("kbl,krl->kbr", part, remap_matrices, precision=HIGH_ACCURACY)
        return jnp.einsum("vrb,vbm->vrm", part, remap_matrices, precision=HIGH_ACCURACY)

    return lax.map(one_group, (rows_grouped, index_grouped)).reshape(
        rows.shape[:2] + (table.shape[2],)
    )


def column_network(latlon, w_in, b_in, w_mid, b_mid, w_out):
    inputs = latlon.astype(jnp.bfloat16)
    first = jnp.einsum("hf,dfc->dhc", w_in, inputs, preferred_element_type=jnp.float32)
    first = jax.nn.gelu(first + b_in[None, :, None], approximate=True).astype(jnp.bfloat16)
    second = jnp.einsum("hk,dkc->dhc", w_mid, first, preferred_element_type=jnp.float32)
    second = jax.nn.gelu(second + b_mid[None, :, None], approximate=True).astype(jnp.bfloat16)
    return jnp.einsum("fh,dhc->dfc", w_out, second, preferred_element_type=jnp.float32)


def diffuse(field, coef):
    cycle = padded(field, (("fx", 2),), 1, True)
    rows = padded(field, (("fy", 0),), 1, False)
    beside_all = cycle[:, :, 2:] + cycle[:, :, :-2] + rows[2:] + rows[:-2]
    return field + coef[:, None, :] * (beside_all - 4.0 * field)


def per_device(
    state,
    coef,
    weight_table,
    src_blocks,
    dst_blocks,
    weight_rows,
    counts,
    brackets,
    fractions,
    w_in,
    b_in,
    w_mid,
    b_mid,
    w_out,
):
    field = state
    for sweep_index in range(SWEEPS):
        field = diffuse(field, coef)
    nblocks, width = (state.shape[0], state.shape[2])
    ndev, cap = (src_blocks.shape[1], src_blocks.shape[2])
    total = ndev * cap
    remap_matrix = level_matrix(brackets, fractions, LEV)
    slots = jnp.arange(cap, dtype=jnp.int32)
    valid = (slots[None, :] < counts[0][:, None]).astype(jnp.float32).reshape(-1)
    flattened_source_rows = src_blocks[0].reshape(-1)
    flat_rows = weight_rows[0].reshape(-1)
    source = apply_levels(field, remap_matrix)
    picked = jnp.take(source, flattened_source_rows, axis=0)
    sent = remap_blocks(picked, flat_rows, weight_table, False) * valid[:, None, None]
    features = sent.shape[1]
    targets = dst_blocks[0].astype(jnp.float32)
    got, got_targets = (
        lax.all_to_all(
            sent.reshape(ndev, cap, features, width),
            ("fx", "fy"),
            split_axis=0,
            concat_axis=0,
            tiled=True,
        ),
        lax.all_to_all(targets, ("fx", "fy"), split_axis=0, concat_axis=0, tiled=True),
    )
    blocks_here = jnp.arange(nblocks, dtype=jnp.float32)
    onehot = (got_targets.reshape(-1)[:, None] == blocks_here[None, :]).astype(jnp.float32)
    latlon = jnp.dot(
        onehot.T, got.reshape(total, features * width), precision=HIGH_ACCURACY
    ).reshape(nblocks, features, width)
    column_tend = column_network(latlon, w_in, b_in, w_mid, b_mid, w_out)
    back = jnp.dot(onehot, column_tend.reshape(nblocks, -1), precision=HIGH_ACCURACY).reshape(
        total, -1, width
    )
    back_features = back.shape[1]
    returned = lax.all_to_all(
        back.reshape(ndev, cap, back_features, width),
        ("fx", "fy"),
        split_axis=0,
        concat_axis=0,
        tiled=True,
    )
    contrib = (
        remap_blocks(returned.reshape(total, back_features, width), flat_rows, weight_table, True)
        * valid[:, None, None]
    )
    contrib = apply_levels(contrib, remap_matrix.T)
    source_hot = (
        flattened_source_rows[:, None] == jnp.arange(nblocks, dtype=jnp.int32)[None, :]
    ).astype(jnp.float32)
    tendency = jnp.dot(source_hot.T, contrib.reshape(total, -1), precision=HIGH_ACCURACY).reshape(
        nblocks, -1, width
    )
    return (field, tendency)


def solution(mesh):
    placed = (
        P("fy", None, "fx"),
        P("fy", "fx"),
        P(),
        P(("fx", "fy"), None, None),
        P(("fx", "fy"), None, None),
        P(("fx", "fy"), None, None),
        P(("fx", "fy"), None),
        P(),
        P(),
        P(),
        P(),
        P(),
        P(),
        P(),
    )
    return jax.shard_map(
        per_device,
        mesh=mesh,
        in_specs=placed,
        out_specs=(P("fy", None, "fx"), P("fy", None, "fx")),
        check_vma=False,
    )
```

profile of v0, /device:TPU:114, one launch (start us, length us, event | category | flops | bytes accessed | tf_op | source)
XLA Modules:
  0.0 766.0 jit_solution(13562779528734940962)
XLA Ops:
  13.7 11.2 %all-to-all-start = ((f32[128,1,4]{2,1,0:T(1,128)}), f32[128,1,4]{2,1,0:T(1,128)S(1)}, u32[]{:S(2)}, u32[]{:S(2)}) async-start(f32[128,1,4]{2,1,0:T(1,128)} %bitcast.7), calls=%async_computation | async-start | bytes 131072 | tf_op jit(solution)/shard_map/all_to_all | solution.py:120
  78.3 8.9 %broadcast_select_fusion = f32[8,64,39,128]{3,2,1,0:T(8,128)} fusion(f32[8,64,39,128]{3,2,1,0:T(8,128)} %bitcast.121, pred[8,64]{1,0:T(8,128)(4,1)S(1)} %compare_and_fusion.2), kind=kLoop, calls=%fused_computation.56 | loop fusion | flops 2555904 | bytes 20447744 | tf_op jit(solution)/shard_map/jit(_take)/select_n | solution.py:108
  87.2 98.9 %while.20 = (s32[]{:T(128)}, f32[8,64,39,128]{3,2,1,0:T(8,128)}, f32[8,64,39,128]{3,2,1,0:T(8,128)}, s32[8,64]{1,0:T(8,128)S(1)}, f32[64,128,128]{2,1,0:T(8,128)}, /*index=5*/s32[]{:T(128)}) while((s32[]{:T(128)}, f32[8,64,39,128]{3,2,1,0:T(8,128)}, f32[8,64,39,128]{3,2,1,0:T(8,128)}, s32[8,64]{1,0:T(8,128)S(1)}, f32[64,128,128]{2,1,0:T(8,128)}, ...), condition=%wide.region_1.3_spmd, body=%wide.region_0.0_spmd.sunk | while | flops 491783552 | bytes 15210697 | solution.py:59
  194.9 10.4 %copy.147 = f32[128,4,39,128]{3,1,2,0:T(4,128)} copy(f32[128,4,39,128]{3,2,1,0:T(8,128)} %broadcast_multiply_fusion) | data formatting | bytes 20447232 | tf_op jit(solution)/shard_map/mul | solution.py:109
  205.3 14.1 %all-to-all-start.1 = ((f32[128,4,39,128]{3,1,2,0:T(4,128)}), f32[128,4,39,128]{3,1,2,0:T(4,128)}, u32[]{:S(2)}, u32[]{:S(2)}) async-start(f32[128,4,39,128]{3,1,2,0:T(4,128)} %copy.147), calls=%async_computation.1 | async-start | bytes 20447232 | tf_op jit(solution)/shard_map/all_to_all | solution.py:113
  221.0 131.0 %all-to-all-done.1 = f32[128,4,39,128]{3,1,2,0:T(4,128)} async-done(((f32[128,4,39,128]{3,1,2,0:T(4,128)}), f32[128,4,39,128]{3,1,2,0:T(4,128)}, u32[]{:S(2)}, u32[]{:S(2)}) %all-to-all-start.1) | async-done | bytes 10223648 | tf_op jit(solution)/shard_map/all_to_all | solution.py:113
  363.0 11.0 %copy.149 = f32[4992,512]{1,0:T(8,128)} copy(f32[4992,512]{0,1:T(8,128)} %bitcast.123) | data formatting | bytes 20447232 | tf_op jit(solution)/shard_map/dot_general | solution.py:124
  401.2 14.4 %copy.153 = f32[128,4,39,128]{3,1,2,0:T(4,128)} copy(f32[128,4,39,128]{3,0,2,1:T(8,128)} %fusion.75) | data formatting | bytes 20447232 | tf_op jit(solution)/shard_map/dot_general | solution.py:128
  415.6 9.0 %all-to-all-start.2 = ((f32[128,4,39,128]{3,1,2,0:T(4,128)}), f32[128,4,39,128]{3,1,2,0:T(4,128)}, u32[]{:S(2)}, u32[]{:S(2)}) async-start(f32[128,4,39,128]{3,1,2,0:T(4,128)} %copy.153), calls=%async_computation.2 | async-start | bytes 20447232 | tf_op jit(solution)/shard_map/all_to_all | solution.py:132
  424.9 132.4 %all-to-all-done.2 = f32[128,4,39,128]{3,1,2,0:T(4,128)} async-done(((f32[128,4,39,128]{3,1,2,0:T(4,128)}), f32[128,4,39,128]{3,1,2,0:T(4,128)}, u32[]{:S(2)}, u32[]{:S(2)}) %all-to-all-start.2) | async-done | bytes 10223648 | tf_op jit(solution)/shard_map/all_to_all | solution.py:132
  557.3 8.9 %copy.154 = f32[128,4,39,128]{3,2,1,0:T(8,128)} copy(f32[128,4,39,128]{3,1,2,0:T(4,128)} %all-to-all-done.2) | data formatting | bytes 20447232 | tf_op jit(solution)/shard_map/all_to_all | solution.py:132
  566.1 135.4 %while.21 = (s32[]{:T(128)}, f32[8,64,39,128]{3,1,0,2:T(8,128)}, f32[8,64,39,128]{3,2,1,0:T(8,128)}, s32[8,64]{1,0:T(8,128)S(1)}, f32[64,128,128]{2,1,0:T(8,128)}, /*index=5*/s32[]{:T(128)}) while((s32[]{:T(128)}, f32[8,64,39,128]{3,1,0,2:T(8,128)}, f32[8,64,39,128]{3,2,1,0:T(8,128)}, s32[8,64]{1,0:T(8,128)S(1)}, f32[64,128,128]{2,1,0:T(8,128)}, ...), condition=%wide.region_3.5_spmd, body=%wide.region_2.4_spmd.sunk | while | flops 491783552 | bytes 17733832 | solution.py:59
  571.2 10.5 %fusion.138 = f32[1,64,39,128]{3,2,1,0:T(8,128)S(1)} fusion(f32[64,128,128]{2,1,0:T(8,128)} %gather_fusion.1, pred[64]{0:T(512)(128)(4,1)S(1)} %get-tuple-element.180, f32[8,64,39,128]{3,2,1,0:T(8,128)} %get-tuple-element.213, s32[]{:T(128)} %get-tuple-element.205), kind=kOutput, calls=%fused_computation.22.clone.1 | convolution fusion | flops 491782144 | bytes 6783552 | tf_op jit(solution)/shard_map/while/body/eval_jaxpr/kbl,krl->kbr/dot_general | solution.py:56
  588.1 10.5 %fusion.138 = f32[1,64,39,128]{3,2,1,0:T(8,128)S(1)} fusion(f32[64,128,128]{2,1,0:T(8,128)} %gather_fusion.1, pred[64]{0:T(512)(128)(4,1)S(1)} %get-tuple-element.180, f32[8,64,39,128]{3,2,1,0:T(8,128)} %get-tuple-element.213, s32[]{:T(128)} %get-tuple-element.205), kind=kOutput, calls=%fused_computation.22.clone.1 | convolution fusion | flops 491782144 | bytes 6783552 | tf_op jit(solution)/shard_map/while/body/eval_jaxpr/kbl,krl->kbr/dot_general | solution.py:56
  605.1 10.5 %fusion.138 = f32[1,64,39,128]{3,2,1,0:T(8,128)S(1)} fusion(f32[64,128,128]{2,1,0:T(8,128)} %gather_fusion.1, pred[64]{0:T(512)(128)(4,1)S(1)} %get-tuple-element.180, f32[8,64,39,128]{3,2,1,0:T(8,128)} %get-tuple-element.213, s32[]{:T(128)} %get-tuple-element.205), kind=kOutput, calls=%fused_computation.22.clone.1 | convolution fusion | flops 491782144 | bytes 6783552 | tf_op jit(solution)/shard_map/while/body/eval_jaxpr/kbl,krl->kbr/dot_general | solution.py:56
  622.0 10.5 %fusion.138 = f32[1,64,39,128]{3,2,1,0:T(8,128)S(1)} fusion(f32[64,128,128]{2,1,0:T(8,128)} %gather_fusion.1, pred[64]{0:T(512)(128)(4,1)S(1)} %get-tuple-element.180, f32[8,64,39,128]{3,2,1,0:T(8,128)} %get-tuple-element.213, s32[]{:T(128)} %get-tuple-element.205), kind=kOutput, calls=%fused_computation.22.clone.1 | convolution fusion | flops 491782144 | bytes 6783552 | tf_op jit(solution)/shard_map/while/body/eval_jaxpr/kbl,krl->kbr/dot_general | solution.py:56
  638.9 10.5 %fusion.138 = f32[1,64,39,128]{3,2,1,0:T(8,128)S(1)} fusion(f32[64,128,128]{2,1,0:T(8,128)} %gather_fusion.1, pred[64]{0:T(512)(128)(4,1)S(1)} %get-tuple-element.180, f32[8,64,39,128]{3,2,1,0:T(8,128)} %get-tuple-element.213, s32[]{:T(128)} %get-tuple-element.205), kind=kOutput, calls=%fused_computation.22.clone.1 | convolution fusion | flops 491782144 | bytes 6783552 | tf_op jit(solution)/shard_map/while/body/eval_jaxpr/kbl,krl->kbr/dot_general | solution.py:56
  655.9 10.5 %fusion.138 = f32[1,64,39,128]{3,2,1,0:T(8,128)S(1)} fusion(f32[64,128,128]{2,1,0:T(8,128)} %gather_fusion.1, pred[64]{0:T(512)(128)(4,1)S(1)} %get-tuple-element.180, f32[8,64,39,128]{3,2,1,0:T(8,128)} %get-tuple-element.213, s32[]{:T(128)} %get-tuple-element.205), kind=kOutput, calls=%fused_computation.22.clone.1 | convolution fusion | flops 491782144 | bytes 6783552 | tf_op jit(solution)/shard_map/while/body/eval_jaxpr/kbl,krl->kbr/dot_general | solution.py:56
  672.8 10.5 %fusion.138 = f32[1,64,39,128]{3,2,1,0:T(8,128)S(1)} fusion(f32[64,128,128]{2,1,0:T(8,128)} %gather_fusion.1, pred[64]{0:T(512)(128)(4,1)S(1)} %get-tuple-element.180, f32[8,64,39,128]{3,2,1,0:T(8,128)} %get-tuple-element.213, s32[]{:T(128)} %get-tuple-element.205), kind=kOutput, calls=%fused_computation.22.clone.1 | convolution fusion | flops 491782144 | bytes 6783552 | tf_op jit(solution)/shard_map/while/body/eval_jaxpr/kbl,krl->kbr/dot_general | solution.py:56
  689.7 10.5 %fusion.138 = f32[1,64,39,128]{3,2,1,0:T(8,128)S(1)} fusion(f32[64,128,128]{2,1,0:T(8,128)} %gather_fusion.1, pred[64]{0:T(512)(128)(4,1)S(1)} %get-tuple-element.180, f32[8,64,39,128]{3,2,1,0:T(8,128)} %get-tuple-element.213, s32[]{:T(128)} %get-tuple-element.205), kind=kOutput, calls=%fused_computation.22.clone.1 | convolution fusion | flops 491782144 | bytes 6783552 | tf_op jit(solution)/shard_map/while/body/eval_jaxpr/kbl,krl->kbr/dot_general | solution.py:56
  707.1 20.2 %fusion.27 = f32[512,3,128,16]{2,3,1,0:T(8,128)} fusion(f32[512,3,13,128]{3,0,2,1:T(8,128)S(1)} %broadcast_multiply_fusion.1, f32[13]{0:T(128)S(1)} %copy-done.4, s32[13]{0:T(128)S(1)} %broadcast_add_fusion, f32[13]{0:T(128)S(1)} %broadcast_subtract_fusion, s32[13]{0:T(128)S(1)} %copy-done.5), kind=kOutput, calls=%fused_computation.34 | convolution fusion | flops 490734592 | bytes 22806736 | tf_op jit(solution)/shard_map/fm,...qme->...qfe/dot_general | solution.py:40
  727.4 14.9 %copy.187 = f32[64,8,48,128]{3,1,2,0:T(8,128)} copy(f32[64,8,48,128]{3,2,1,0:T(8,128)} %bitcast.117) | data formatting | bytes 25165824
  742.3 12.7 %copy.157 = f32[6144,512]{1,0:T(8,128)} copy(f32[6144,512]{0,1:T(8,128)} %bitcast.119) | data formatting | bytes 25165824 | tf_op jit(solution)/shard_map/dot_general | solution.py:147
  755.0 9.2 %fusion.81 = f32[32,48,128]{2,0,1:T(8,128)S(1)} fusion(f32[48,128,512]{2,1,0:T(8,128)} %bitcast.118, s32[512]{0:T(512)S(1)} %eq.82), kind=kOutput, calls=%fused_computation.114 | convolution fusion | flops 1207975936 | bytes 13371392 | tf_op jit(solution)/shard_map/dot_general | solution.py:147
  (181 shorter events, 271.3 us)
Async XLA Ops:
  0.6 381.0 %copy-start = (bf16[512,512]{1,0:T(8,128)(2,1)S(1)}, bf16[512,512]{1,0:T(8,128)(2,1)}, u32[]{:S(2)}) copy-start(bf16[512,512]{1,0:T(8,128)(2,1)} %param.31) | copy-start | bytes 1572868
  0.6 42.3 %copy-start.3 = (f32[32,128]{1,0:T(8,128)S(1)}, f32[32,128]{1,0:T(8,128)}, u32[]{:S(2)}) copy-start(f32[32,128]{1,0:T(8,128)} %param.21) | copy-start | bytes 49156
  0.7 39.6 %copy-start.5 = (s32[13]{0:T(128)S(1)}, s32[13]{0:T(128)}, u32[]{:S(2)}) copy-start(s32[13]{0:T(128)} %param.27) | copy-start | bytes 160
  2.7 24.0 %collective-permute-start = (f32[32,48,1]{1,0,2:T(8,128)S(1)}, f32[32,48,1]{1,0,2:T(8,128)S(1)}, u32[]{:S(2)}, u32[]{:S(2)}) collective-permute-start(f32[32,48,1]{1,0,2:T(8,128)S(1)} %copy.166), channel_id=1, source_target_pairs={{8,0},{16,8},{24,16},{32,24},{40,32},{48,40},{56,48},{64,56},{72,6... | collective-permute-start | bytes 18440 | tf_op jit(solution)/shard_map/ppermute | solution.py:23
  3.4 23.6 %collective-permute-start.1 = (f32[32,48,1]{1,0,2:T(8,128)S(1)}, f32[32,48,1]{1,0,2:T(8,128)S(1)}, u32[]{:S(2)}, u32[]{:S(2)}) collective-permute-start(f32[32,48,1]{1,0,2:T(8,128)S(1)} %copy.167), channel_id=1, source_target_pairs={{0,8},{8,16},{16,24},{24,32},{32,40},{40,48},{48,56},{56,64},{64,7... | collective-permute-start | bytes 18440 | tf_op jit(solution)/shard_map/ppermute | solution.py:20
  8.0 19.4 %collective-permute-start.2 = (f32[1,48,128]{2,1,0:T(8,128)S(1)}, f32[1,48,128]{2,1,0:T(8,128)S(1)}, u32[]{:S(2)}, u32[]{:S(2)}) collective-permute-start(f32[1,48,128]{2,1,0:T(8,128)S(1)} %get-tuple-element.109), channel_id=1, source_target_pairs={{1,0},{2,1},{3,2},{4,3},{5,4},{6,5},{7,6},{9,8},{10,9},{11,10},{12... | collective-permute-start | bytes 73736 | tf_op jit(solution)/shard_map/ppermute | solution.py:23
  9.9 17.5 %collective-permute-start.3 = (f32[1,48,128]{2,1,0:T(8,128)S(1)}, f32[1,48,128]{2,1,0:T(8,128)S(1)}, u32[]{:S(2)}, u32[]{:S(2)}) collective-permute-start(f32[1,48,128]{2,1,0:T(8,128)S(1)} %get-tuple-element.110), channel_id=1, source_target_pairs={{0,1},{1,2},{2,3},{3,4},{4,5},{5,6},{6,7},{8,9},{9,10},{10,11},{11... | collective-permute-start | bytes 73736 | tf_op jit(solution)/shard_map/ppermute | solution.py:20
  13.7 191.5 %all-to-all-start = ((f32[128,1,4]{2,1,0:T(1,128)}), f32[128,1,4]{2,1,0:T(1,128)S(1)}, u32[]{:S(2)}, u32[]{:S(2)}) async-start(f32[128,1,4]{2,1,0:T(1,128)} %bitcast.7), calls=%async_computation | async-start | bytes 131072 | tf_op jit(solution)/shard_map/all_to_all | solution.py:120
  27.4 26.8 %copy-start.4 = (f32[13]{0:T(128)S(1)}, f32[13]{0:T(128)}, u32[]{:S(2)}) copy-start(f32[13]{0:T(128)} %param.28) | copy-start | bytes 160
  31.3 8.9 %collective-permute-start.4 = (f32[32,48,1]{1,0,2:T(8,128)S(1)}, f32[32,48,1]{1,0,2:T(8,128)S(1)}, u32[]{:S(2)}, u32[]{:S(2)}) collective-permute-start(f32[32,48,1]{1,0,2:T(8,128)S(1)} %copy.126), channel_id=1, source_target_pairs={{8,0},{16,8},{24,16},{32,24},{40,32},{48,40},{56,48},{64,56},{72,6... | collective-permute-start | bytes 18440 | tf_op jit(solution)/shard_map/ppermute | solution.py:23
  32.3 8.3 %collective-permute-start.5 = (f32[32,48,1]{1,0,2:T(8,128)S(1)}, f32[32,48,1]{1,0,2:T(8,128)S(1)}, u32[]{:S(2)}, u32[]{:S(2)}) collective-permute-start(f32[32,48,1]{1,0,2:T(8,128)S(1)} %copy.128), channel_id=1, source_target_pairs={{0,8},{8,16},{16,24},{24,32},{32,40},{40,48},{48,56},{56,64},{64,7... | collective-permute-start | bytes 18440 | tf_op jit(solution)/shard_map/ppermute | solution.py:20
  35.9 5.9 collective-permute-start.6
  37.8 5.1 collective-permute-start.7
  41.8 26.7 %copy-start.6 = (s32[1,128,4]{1,2,0:T(4,128)S(1)}, s32[1,128,4]{1,2,0:T(4,128)}, u32[]{:S(2)}) copy-start(s32[1,128,4]{1,2,0:T(4,128)} %param.25) | copy-start | bytes 6148
  45.4 8.9 %collective-permute-start.8 = (f32[32,48,1]{1,0,2:T(8,128)S(1)}, f32[32,48,1]{1,0,2:T(8,128)S(1)}, u32[]{:S(2)}, u32[]{:S(2)}) collective-permute-start(f32[32,48,1]{1,0,2:T(8,128)S(1)} %copy.130), channel_id=1, source_target_pairs={{8,0},{16,8},{24,16},{32,24},{40,32},{48,40},{56,48},{64,56},{72,6... | collective-permute-start | bytes 18440 | tf_op jit(solution)/shard_map/ppermute | solution.py:23
  45.7 8.9 %collective-permute-start.9 = (f32[32,48,1]{1,0,2:T(8,128)S(1)}, f32[32,48,1]{1,0,2:T(8,128)S(1)}, u32[]{:S(2)}, u32[]{:S(2)}) collective-permute-start(f32[32,48,1]{1,0,2:T(8,128)S(1)} %copy.132), channel_id=1, source_target_pairs={{0,8},{8,16},{16,24},{24,32},{32,40},{40,48},{48,56},{56,64},{64,7... | collective-permute-start | bytes 18440 | tf_op jit(solution)/shard_map/ppermute | solution.py:20
  49.9 5.9 collective-permute-start.10
  51.8 5.1 collective-permute-start.11
  59.4 9.3 %collective-permute-start.12 = (f32[32,48,1]{1,0,2:T(8,128)S(1)}, f32[32,48,1]{1,0,2:T(8,128)S(1)}, u32[]{:S(2)}, u32[]{:S(2)}) collective-permute-start(f32[32,48,1]{1,0,2:T(8,128)S(1)} %copy.134), channel_id=1, source_target_pairs={{8,0},{16,8},{24,16},{32,24},{40,32},{48,40},{56,48},{64,56},{72,6... | collective-permute-start | bytes 18440 | tf_op jit(solution)/shard_map/ppermute | solution.py:23
  59.8 9.3 %collective-permute-start.13 = (f32[32,48,1]{1,0,2:T(8,128)S(1)}, f32[32,48,1]{1,0,2:T(8,128)S(1)}, u32[]{:S(2)}, u32[]{:S(2)}) collective-permute-start(f32[32,48,1]{1,0,2:T(8,128)S(1)} %copy.136), channel_id=1, source_target_pairs={{0,8},{8,16},{16,24},{24,32},{32,40},{40,48},{48,56},{56,64},{64,7... | collective-permute-start | bytes 18440 | tf_op jit(solution)/shard_map/ppermute | solution.py:20
  63.9 5.5 collective-permute-start.14
  65.9 5.1 collective-permute-start.15
  205.3 146.7 %all-to-all-start.1 = ((f32[128,4,39,128]{3,1,2,0:T(4,128)}), f32[128,4,39,128]{3,1,2,0:T(4,128)}, u32[]{:S(2)}, u32[]{:S(2)}) async-start(f32[128,4,39,128]{3,1,2,0:T(4,128)} %copy.147), calls=%async_computation.1 | async-start | bytes 20447232 | tf_op jit(solution)/shard_map/all_to_all | solution.py:113
  415.6 141.6 %all-to-all-start.2 = ((f32[128,4,39,128]{3,1,2,0:T(4,128)}), f32[128,4,39,128]{3,1,2,0:T(4,128)}, u32[]{:S(2)}, u32[]{:S(2)}) async-start(f32[128,4,39,128]{3,1,2,0:T(4,128)} %copy.153), calls=%async_computation.2 | async-start | bytes 20447232 | tf_op jit(solution)/shard_map/all_to_all | solution.py:132
  (6 other events, 54.2 us)
where the time goes:
time: 775 us; the launch traced here: 766 us
  waiting for transfers between devices  267 us (34%)
  matrix products  200 us (26%)
  local copies, waits for them, and re-layouts  195 us (25%)
  starting transfers between devices  68.9 us (9%)
  other arithmetic  33.4 us (4%)
    all_to_all x1, waiting for transfers between devices, per_device(): lax.all_to_all(back.reshape(ndev, cap, back_features, width), ('fx', 'fy'...  132 us
    all_to_all x1, waiting for transfers between devices, per_device(): lax.all_to_all(sent.reshape(ndev, cap, features, width), ('fx', 'fy'), sp...  131 us
    dot_general x8, matrix products, one_group(): jnp.einsum('kbl,krl->kbr', part, remap_matrices, precision=HIGH_ACCURACY)  84.4 us
    gather x16, local copies, waits for them, and re-layouts, one_group(): remap_matrices = jnp.take(table, index, axis=0)  80.5 us
    dot_general x8, matrix products, one_group(): jnp.einsum('vrb,vbm->vrm', part, remap_matrices, precision=HIGH_ACCURACY)  58.3 us
    ppermute x8, starting transfers between devices, padded(): lax.ppermute(lax.slice_in_dim(block, block.shape[dim] - width, None, axis...  25.6 us
    unnamed x30, local copies, waits for them, and re-layouts  24.8 us
    dot_general x2, matrix products, apply_levels(): jnp.einsum('fm,...qme->...qfe', remap_matrix, divided_parts, precision=HI...  21.1 us
  transfers between devices with their start and end apart: 19, of which 5 were waited for; matrix products, arithmetic and copies ran while one was open for 20% of the time, Pallas kernels for 0%

commit v1 on v0

v1 whole, which is shorter than its diff:
```python
import functools

import jax
import jax.numpy as jnp
from jax import lax
from jax.experimental import pallas as pl
from jax.experimental.pallas import tpu as pltpu
from jax.sharding import PartitionSpec as P

SWEEPS = 4
VMEM_LIMIT = 48 * 1024 * 1024
F32 = jnp.float32
BF16 = jnp.bfloat16
HIGHEST = lax.Precision.HIGHEST

VMEM_SPEC = pl.BlockSpec(memory_space=pltpu.VMEM)
SMEM_SPEC = pl.BlockSpec(memory_space=pltpu.SMEM)


def params():
    return pltpu.CompilerParams(vmem_limit_bytes=VMEM_LIMIT)


def pack_kernel(nrows, nlev, width, state, coef, top, bottom, first_out, last_out):
    halo = SWEEPS
    lane = lax.broadcasted_iota(jnp.int32, (nlev, width), 1)
    group = lane // halo
    lane_one = lax.broadcasted_iota(jnp.int32, (1, width), 1)
    group_one = lane_one // halo

    def rows_of(e):
        if e < halo:
            return top[e * nlev : (e + 1) * nlev, :], top[halo * nlev + e : halo * nlev + e + 1, :]
        if e < halo + nrows:
            return state[e - halo], coef[e - halo : e - halo + 1, :]
        b = e - halo - nrows
        return bottom[b * nlev : (b + 1) * nlev, :], bottom[halo * nlev + b : halo * nlev + b + 1, :]

    per = width // halo
    total = nrows + 2 * halo
    tiles = -(-total // per)
    first_out[...] = jnp.zeros_like(first_out)
    last_out[...] = jnp.zeros_like(last_out)
    for tile in range(tiles):
        first = jnp.zeros((nlev, width), F32)
        last = jnp.zeros((nlev, width), F32)
        first_c = jnp.zeros((1, width), F32)
        last_c = jnp.zeros((1, width), F32)
        for i in range(min(per, total - tile * per)):
            field, number = rows_of(tile * per + i)
            at = (halo * i) % width
            up = (halo * i + halo) % width
            first = jnp.where(group == i, pltpu.roll(field, at, 1) if at else field, first)
            last = jnp.where(group == i, pltpu.roll(field, up, 1) if up else field, last)
            first_c = jnp.where(group_one == i, pltpu.roll(number, at, 1) if at else number, first_c)
            last_c = jnp.where(group_one == i, pltpu.roll(number, up, 1) if up else number, last_c)
        first_out[tile * nlev : (tile + 1) * nlev, :] = first
        last_out[tile * nlev : (tile + 1) * nlev, :] = last
        first_out[tiles * nlev + tile : tiles * nlev + tile + 1, :] = first_c
        last_out[tiles * nlev + tile : tiles * nlev + tile + 1, :] = last_c


def sweep_kernel(
    nrows, nlev, width, state, coef, top, bottom, left, right, levels, field_out, source_out, a, b, c
):
    halo = SWEEPS
    per = width // halo
    total = nrows + 2 * halo
    tiles = -(-total // per)
    lane = lax.broadcasted_iota(jnp.int32, (nlev, width), 1)
    lane_one = lax.broadcasted_iota(jnp.int32, (1, width), 1)
    for e in range(total):
        if e < halo:
            field = top[e * nlev : (e + 1) * nlev, :]
            number = top[halo * nlev + e : halo * nlev + e + 1, :]
        elif e < halo + nrows:
            field = state[e - halo]
            number = coef[e - halo : e - halo + 1, :]
        else:
            r = e - halo - nrows
            field = bottom[r * nlev : (r + 1) * nlev, :]
            number = bottom[halo * nlev + r : halo * nlev + r + 1, :]
        tile, i = e // per, e % per
        to_low = (width - halo * i) % width
        to_high = (width - halo - halo * i) % width
        edges = []
        for where_, rows in ((lane, slice(tile * nlev, (tile + 1) * nlev)),
                             (lane_one, slice(tiles * nlev + tile, tiles * nlev + tile + 1))):
            r_tile = right[rows, :]
            l_tile = left[rows, :]
            r_part = pltpu.roll(r_tile, to_low, 1) if to_low else r_tile
            l_part = pltpu.roll(l_tile, to_high, 1) if to_high else l_tile
            edges.append(
                jnp.where(where_ < halo, r_part, jnp.where(where_ >= width - halo, l_part, 0.0))
            )
        a[e, :, 0:width] = field
        a[e, :, width : 2 * width] = edges[0]
        c[e, :, 0:width] = number
        c[e, :, width : 2 * width] = edges[1]

    def step(source, e):
        mid = source[e]
        beside = pltpu.roll(mid, 1, 1) + pltpu.roll(mid, 2 * width - 1, 1)
        beside = beside + source[e + 1] + source[e - 1]
        return mid + c[e] * (beside - 4.0 * mid)

    held, other = a, b
    for sweep in range(1, SWEEPS):

        def one(e, carry, held=held, other=other):
            other[e] = step(held, e)
            return carry

        lax.fori_loop(sweep, total - sweep, one, 0)
        held, other = other, held

    def final(r, carry):
        done = step(held, r + halo)[:, 0:width]
        field_out[r] = done
        source_out[r] = jnp.dot(
            levels[...], done, precision=HIGHEST, preferred_element_type=F32
        )
        return carry

    lax.fori_loop(0, nrows, final, 0)


def diffuse(state, coef, levels):
    nrows, nlev, width = state.shape
    halo = SWEEPS
    per = width // halo
    total = nrows + 2 * halo
    tiles = -(-total // per)
    nx, ny = lax.axis_size("fx"), lax.axis_size("fy")
    pad = -halo % 8
    blank = jnp.zeros((pad, width), F32)

    def row_message(rows):
        return jnp.concatenate(
            [state[rows].reshape(halo * nlev, width), coef[rows], blank], axis=0
        )

    down = [(i, i + 1) for i in range(ny - 1)]
    up = [(i + 1, i) for i in range(ny - 1)]
    top = lax.ppermute(row_message(slice(nrows - halo, nrows)), "fy", down)
    bottom = lax.ppermute(row_message(slice(0, halo)), "fy", up)
    edge = jax.ShapeDtypeStruct((tiles * nlev + 8, width), F32)
    first, last = pl.pallas_call(
        functools.partial(pack_kernel, nrows, nlev, width),
        out_shape=(edge, edge),
        in_specs=[VMEM_SPEC] * 4,
        out_specs=(VMEM_SPEC, VMEM_SPEC),
        compiler_params=params(),
        name="pack_edges",
    )(state, coef, top, bottom)
    ahead = [(i, (i + 1) % nx) for i in range(nx)]
    behind = [((i + 1) % nx, i) for i in range(nx)]
    left = lax.ppermute(last, "fx", ahead)
    right = lax.ppermute(first, "fx", behind)
    return pl.pallas_call(
        functools.partial(sweep_kernel, nrows, nlev, width),
        out_shape=(
            jax.ShapeDtypeStruct(state.shape, F32),
            jax.ShapeDtypeStruct((nrows, levels.shape[0], width), F32),
        ),
        in_specs=[VMEM_SPEC] * 7,
        out_specs=(VMEM_SPEC, VMEM_SPEC),
        scratch_shapes=[
            pltpu.VMEM((total, nlev, 2 * width), F32),
            pltpu.VMEM((total, nlev, 2 * width), F32),
            pltpu.VMEM((total, 1, 2 * width), F32),
        ],
        compiler_params=params(),
        name="sweeps",
    )(state, coef, top, bottom, left, right, levels)


def split(value):
    high = value.astype(BF16)
    low = (value - high.astype(F32)).astype(BF16)
    return high, low


def table_kernel(table, plain, turned):
    for k in range(table.shape[0]):
        weights = table[k]
        high, low = split(weights)
        plain[k, :, 0:128] = high
        plain[k, :, 128:256] = low
        high, low = split(weights.T)
        turned[k, :, 0:128] = high
        turned[k, :, 128:256] = low


def split_tables(table):
    count, rows, width = table.shape
    group = 8
    shape = jax.ShapeDtypeStruct((count, rows, 2 * width), BF16)
    return pl.pallas_call(
        table_kernel,
        grid=(count // group,),
        out_shape=(shape, shape),
        in_specs=[pl.BlockSpec((group, rows, width), lambda i: (i, 0, 0))],
        out_specs=(
            pl.BlockSpec((group, rows, 2 * width), lambda i: (i, 0, 0)),
            pl.BlockSpec((group, rows, 2 * width), lambda i: (i, 0, 0)),
        ),
        compiler_params=params(),
        name="split_tables",
    )(table)


UNROLL = 4


def list_kernel(groups, owners, cap, blocks, takes, gives, rows, counts, from_, to, which, number):
    def pair(i, at):
        g = i // owners
        o = i % owners
        for c in range(cap):
            from_[at + c] = g * blocks + takes[i, c]
            to[at + c] = o * blocks + gives[i, c]
            which[at + c] = rows[i, c]
        return at + counts[i, 0]

    end = lax.fori_loop(0, groups * owners, pair, 0)
    for c in range(UNROLL):
        from_[end + c] = 0
        to[end + c] = owners * blocks
        which[end + c] = 0
    number[0] = (end + UNROLL - 1) // UNROLL


def slot_list(takes, gives, rows, counts, blocks):
    groups, owners, cap = takes.shape
    size = groups * owners * cap + 2 * UNROLL
    one = jax.ShapeDtypeStruct((size,), jnp.int32)
    pairs = groups * owners
    return pl.pallas_call(
        functools.partial(list_kernel, groups, owners, cap, blocks),
        out_shape=(one, one, one, jax.ShapeDtypeStruct((1,), jnp.int32)),
        in_specs=[SMEM_SPEC] * 4,
        out_specs=(SMEM_SPEC,) * 4,
        name="slot_list",
    )(
        takes.reshape(pairs, cap),
        gives.reshape(pairs, cap),
        rows.reshape(pairs, cap),
        counts.reshape(pairs, 1),
    )


def remap_kernel(number, from_, to, which, blocks, tables, out, total):
    features, width = blocks.shape[1:]
    total[...] = jnp.zeros_like(total)

    def group(i, carry):
        products = []
        for u in range(UNROLL):
            s = i * UNROLL + u
            value = blocks[from_[s]]
            high = value.astype(BF16).astype(F32)
            both = jnp.concatenate([high, value - high], axis=0).astype(BF16)
            r = jnp.dot(both, tables[which[s]], preferred_element_type=F32)
            products.append(
                r[:features, :width] + r[:features, width:] + r[features:, :width]
            )
        for u in range(UNROLL):
            t = to[i * UNROLL + u]
            total[t] = total[t] + products[u]
        return carry

    lax.fori_loop(0, number[0], group, 0)
    out[...] = total[0 : out.shape[0]]


def remap(slots, blocks, tables, count):
    from_, to, which, number = slots
    shape = (count,) + blocks.shape[1:]
    return pl.pallas_call(
        remap_kernel,
        out_shape=jax.ShapeDtypeStruct(shape, F32),
        in_specs=[SMEM_SPEC] * 4 + [VMEM_SPEC] * 2,
        out_specs=VMEM_SPEC,
        scratch_shapes=[pltpu.VMEM((count + 1,) + blocks.shape[1:], F32)],
        compiler_params=params(),
        name="remap",
    )(number, from_, to, which, blocks, tables)


def gelu(x):
    inner = x * (0.7978845608028654 + (0.7978845608028654 * 0.044715) * (x * x))
    half = 0.5 * x
    return half + half * jnp.tanh(inner)


def network_kernel(latlon, w_in, b_in, w_mid, b_mid, w_out, out):
    def pair(i, carry):
        x = jnp.concatenate([latlon[2 * i], latlon[2 * i + 1]], axis=1).astype(BF16)
        first = jnp.dot(w_in[...], x, preferred_element_type=F32) + b_in[...]
        first = gelu(first).astype(BF16)
        second = jnp.dot(w_mid[...], first, preferred_element_type=F32) + b_mid[...]
        second = gelu(second).astype(BF16)
        tend = jnp.dot(w_out[...], second, preferred_element_type=F32)
        width = latlon.shape[2]
        out[2 * i] = tend[:, :width]
        out[2 * i + 1] = tend[:, width:]
        return carry

    lax.fori_loop(0, latlon.shape[0] // 2, pair, 0)


def column_network(latlon, w_in, b_in, w_mid, b_mid, w_out):
    return pl.pallas_call(
        network_kernel,
        out_shape=jax.ShapeDtypeStruct(latlon.shape, F32),
        in_specs=[VMEM_SPEC] * 6,
        out_specs=VMEM_SPEC,
        compiler_params=params(),
        name="column_network",
    )(latlon, w_in, b_in[:, None], w_mid, b_mid[:, None], w_out)


def raise_kernel(values, levels, out):
    for b in range(values.shape[0]):
        out[b] = jnp.dot(levels[...], values[b], precision=HIGHEST, preferred_element_type=F32)


def raise_levels(values, levels):
    return pl.pallas_call(
        raise_kernel,
        out_shape=jax.ShapeDtypeStruct(
            (values.shape[0], levels.shape[0], values.shape[2]), F32
        ),
        in_specs=[VMEM_SPEC] * 2,
        out_specs=VMEM_SPEC,
        compiler_params=params(),
        name="raise_levels",
    )(values, levels)


def level_matrix(brackets, fractions, nlev, variables, features):
    levels = nlev // variables
    cols = jnp.arange(levels, dtype=jnp.int32)
    lower = (cols[None, :] == brackets[:, None]).astype(F32)
    upper = (cols[None, :] == brackets[:, None] + 1).astype(F32)
    one = lower * (1.0 - fractions[:, None]) + upper * fractions[:, None]
    whole = (jnp.eye(variables, dtype=F32)[:, None, :, None] * one[None, :, None, :]).reshape(
        variables * one.shape[0], nlev
    )
    return jnp.pad(whole, ((0, features - whole.shape[0]), (0, 0)))


def per_device(
    state,
    coef,
    weight_table,
    src_blocks,
    dst_blocks,
    weight_rows,
    counts,
    brackets,
    fractions,
    w_in,
    b_in,
    w_mid,
    b_mid,
    w_out,
):
    nblocks, nlev, width = state.shape
    used_features = w_in.shape[1]
    features = -(-used_features // 8) * 8
    variables = used_features // brackets.shape[0]
    nx, ny = lax.axis_size("fx"), lax.axis_size("fy")
    mx, my = lax.axis_index("fx"), lax.axis_index("fy")
    ndev, cap = src_blocks.shape[1:]

    levels = level_matrix(brackets, fractions, nlev, variables, features)
    lists = jnp.concatenate(
        [src_blocks[0], dst_blocks[0], weight_rows[0], counts[0][:, None]], axis=1
    )
    along_x = lax.all_gather(lists, "fx", axis=0).reshape(nx, nx, ny, 3 * cap + 1)
    along_x = lax.dynamic_index_in_dim(along_x, mx, 1, keepdims=False)
    along_y = lax.all_gather(lists, "fy", axis=0).reshape(ny, nx, ny, 3 * cap + 1)
    along_y = lax.dynamic_index_in_dim(along_y, my, 2, keepdims=False)

    def parts(t):
        return t[..., :cap], t[..., cap : 2 * cap], t[..., 2 * cap : 3 * cap], t[..., 3 * cap]

    src, dst, row, cnt = parts(along_x)
    out_slots = slot_list(src, dst, row, cnt, nblocks)
    src, dst, row, cnt = (jnp.swapaxes(t, 0, 1) for t in parts(along_y))
    back_slots = slot_list(dst, src, row, cnt, nblocks)
    plain, turned = split_tables(weight_table)

    field, source = diffuse(state, coef, levels)
    gathered = lax.all_gather(source, "fx", axis=0, tiled=True)
    sums = remap(out_slots, gathered, plain, ny * nblocks)
    latlon = lax.psum_scatter(sums, "fy", scatter_dimension=0, tiled=True)
    spare = features - used_features
    tend = column_network(
        latlon,
        jnp.pad(w_in, ((0, 0), (0, spare))),
        b_in,
        w_mid,
        b_mid,
        jnp.pad(w_out, ((0, spare), (0, 0))),
    )
    back = lax.all_gather(tend, "fx", axis=0, tiled=True)
    sums = remap(back_slots, back, turned, ny * nblocks)
    returned = lax.psum_scatter(sums, "fy", scatter_dimension=0, tiled=True)
    return field, raise_levels(returned, levels.T)


def solution(mesh):
    placed = (
        P("fy", None, "fx"),
        P("fy", "fx"),
        P(),
        P(("fx", "fy"), None, None),
        P(("fx", "fy"), None, None),
        P(("fx", "fy"), None, None),
        P(("fx", "fy"), None),
        P(),
        P(),
        P(),
        P(),
        P(),
        P(),
        P(),
    )
    return jax.shard_map(
        per_device,
        mesh=mesh,
        in_specs=placed,
        out_specs=(P("fy", None, "fx"), P("fy", None, "fx")),
        check_vma=False,
    )
```

time: 775 us -> 375 us (0.48)
  the two profiles are of different devices: /device:TPU:114 before, /device:TPU:16 now
where the time goes in v1:
time: 375 us; the launch traced here: 374 us
  waiting for transfers between devices  176 us (47%)
  Pallas kernels  107 us (29%)
  blocking collectives  37.2 us (10%)
  local copies, waits for them, and re-layouts  29.1 us (8%)
  between operations  14 us (4%)
  starting transfers between devices  7.4 us (2%)
    all_gather x1, waiting for transfers between devices, per_device(): back = lax.all_gather(tend, 'fx', axis=0, tiled=True)  53.4 us
    pallas_call x2, Pallas kernels, remap(): pl.pallas_call(remap_kernel, out_shape=jax.ShapeDtypeStruct(shape, F32),...  46.7 us
    reduce_scatter x1, waiting for transfers between devices, per_device(): returned = lax.psum_scatter(sums, 'fy', scatter_dimension=0, tiled=True)  41.1 us
    reduce_scatter x1, waiting for transfers between devices, per_device(): latlon = lax.psum_scatter(sums, 'fy', scatter_dimension=0, tiled=True)  39.8 us
    all_gather x1, waiting for transfers between devices, per_device(): gathered = lax.all_gather(source, 'fx', axis=0, tiled=True)  39.2 us
    all_gather x1, blocking collectives, per_device(): lax.all_gather(lists, 'fx', axis=0).reshape(nx, nx, ny, 3 * cap + 1)  24.4 us
    pallas_call x1, Pallas kernels, diffuse(): pl.pallas_call(functools.partial(sweep_kernel, nrows, nlev, width), out_s...  21 us
    unnamed x42, local copies, waits for them, and re-layouts  17.2 us
  transfers between devices with their start and end apart: 8, of which 6 were waited for; matrix products, arithmetic and copies ran while one was open for 4% of the time, Pallas kernels for 6%

profile of v1, /device:TPU:16, one launch (start us, length us, event | category | flops | bytes accessed | tf_op | source)
XLA Modules:
  0.0 374.0 jit_solution(17158472293205318497)
XLA Ops:
  9.1 1.7 collective-permute-start
  10.8 1.3 collective-permute-start.1
  17.8 2.0 collective-permute-start.2
  19.8 2.2 collective-permute-start.3
  22.3 1.7 collective-permute-done.2.left
  24.1 1.1 copy-done.4
  26.0 21.0 %sweeps.1 = (f32[32,48,128]{2,1,0:T(8,128)}, f32[32,40,128]{2,1,0:T(8,128)}) custom-call(f32[32,48,128]{2,1,0:T(8,128)S(1)} %copy-done.4, f32[32,128]{1,0:T(8,128)S(1)} %copy-done.9, f32[200,128]{1,0:T(8,128)S(1)} %collective-permute-done.top, f32[200,128]{1,0:T(8,128)S(1)} %collective-permute-done.1.bottom, f32[104,128]{1,0:T(8,128)S(1)} %collective-permute-done.2.left, ...), custom_call_target="tpu_custom_call" | custom-call | tf_op jit(solution)/shard_map/sweeps/pallas_call | solution.py:160
  47.8 24.4 %all-gather.1 = s32[2048,13]{0,1:T(8,128)S(1)} all-gather(s32[128,13]{0,1:T(8,128)S(1)} %pad_add_fusion), channel_id=3, replica_groups=mesh['fx'=16,'fy'=8] {'fx'}, dimensions={0}, use_global_device_ids=true | all-gather | bytes 113152 | tf_op jit(solution)/shard_map/all_gather | solution.py:382
  76.3 7.3 %split_tables.1 = (bf16[64,128,256]{2,1,0:T(8,128)(2,1)S(1)}, bf16[64,128,256]{2,1,0:T(8,128)(2,1)}) custom-call(f32[64,128,128]{2,1,0:T(8,128)} %table.1), custom_call_target="tpu_custom_call" | custom-call | tf_op jit(solution)/shard_map/split_tables/pallas_call | solution.py:199
  83.6 2.0 copy-done.1
  85.6 8.5 %slot_list.3 = (s32[520]{0:T(1024)}, s32[520]{0:T(1024)}, s32[520]{0:T(1024)}, s32[1]{0:T(128)}) custom-call(s32[128,4]{1,0:T(8,128)} %bitcast.40, s32[128,4]{1,0:T(8,128)} %bitcast.41, s32[128,4]{1,0:T(8,128)} %bitcast.42, s32[128,1]{1,0:T(8,128)} %reshape_squeeze.4.counts), custom_call_target="tpu_custom_call" | custom-call | tf_op jit(solution)/shard_map/slot_list/pallas_call | solution.py:239
  94.1 39.2 %all-gather.5.cloned.1.call-done.blocks = f32[512,40,128]{2,1,0:T(8,128)} async-done(((f32[32,40,128]{2,1,0:T(8,128)}), f32[512,40,128]{2,1,0:T(8,128)}) %all-gather.5.cloned.1.call-update) | async-done | bytes 10485776 | tf_op jit(solution)/shard_map/all_gather | solution.py:397
  133.3 2.2 copy-done.2
  137.5 23.0 %remap.2 = f32[256,40,128]{2,1,0:T(8,128)} custom-call(s32[1]{0:T(128)} %get-tuple-element.23.number, s32[520]{0:T(1024)S(1)} %copy-done.13, s32[520]{0:T(1024)S(1)} %copy-done.14, s32[520]{0:T(1024)S(1)} %copy-done.15, f32[512,40,128]{2,1,0:T(8,128)} %all-gather.5.cloned.1.call-done.blocks, bf16[64,128,256]{2,1,0:T(8,128)(2,1)S(1)} %copy-done.2), custom_call_target="tpu_custom_call" | custom-call | tf_op jit(solution)/shard_map/remap/pallas_call | solution.py:280
  161.7 39.8 %reduce-scatter.3.cloned.1.call-done.latlon = f32[32,40,128]{2,1,0:T(8,128)} async-done(((f32[256,40,128]{2,1,0:T(8,128)}), f32[32,40,128]{2,1,0:T(8,128)}) %reduce-scatter.3.cloned.1.call-update) | async-done | bytes 655376 | tf_op jit(solution)/shard_map/reduce_scatter | solution.py:399
  202.5 12.7 %column_network.1 = f32[32,40,128]{2,1,0:T(8,128)} custom-call(f32[32,40,128]{2,1,0:T(8,128)S(1)} %copy-done.6, bf16[512,40]{1,0:T(8,128)(2,1)S(1)} %pad.13.w_in, f32[512,1]{1,0:T(8,128)S(1)} %copy.68.b_in, bf16[512,512]{1,0:T(8,128)(2,1)S(1)} %copy-done.7, f32[512,1]{1,0:T(8,128)S(1)} %copy.69.b_mid, bf16[40,512]{1,0:T(8,128)(2,1)S(1)} %pad.14.w_out), custom_call_target="tpu_custom_call" | custom-call | tf_op jit(solution)/shard_map/column_network/pallas_call | solution.py:314
  215.3 12.8 %all-gather = s32[1024,13]{0,1:T(8,128)S(1)} all-gather(s32[128,13]{0,1:T(8,128)S(1)} %pad_add_fusion), channel_id=2, replica_groups=mesh['fx'=16,'fy'=8] {'fy'}, dimensions={0}, use_global_device_ids=true | all-gather | bytes 59904 | tf_op jit(solution)/shard_map/all_gather | solution.py:384
  228.6 2.1 dynamic-slice_reduce_fusion
  233.7 8.5 %slot_list.2 = (s32[520]{0:T(1024)}, s32[520]{0:T(1024)}, s32[520]{0:T(1024)}, s32[1]{0:T(128)}) custom-call(s32[128,4]{1,0:T(8,128)} %bitcast.38, s32[128,4]{1,0:T(8,128)} %bitcast.39, s32[128,4]{1,0:T(8,128)} %bitcast.37, s32[128,1]{1,0:T(8,128)} %reshape.127.counts), custom_call_target="tpu_custom_call" | custom-call | tf_op jit(solution)/shard_map/slot_list/pallas_call | solution.py:239
  242.2 53.4 %all-gather.7.cloned.1.call-done.blocks = f32[512,40,128]{2,1,0:T(8,128)} async-done(((f32[32,40,128]{2,1,0:T(8,128)}), f32[512,40,128]{2,1,0:T(8,128)}) %all-gather.7.cloned.1.call-update) | async-done | bytes 10485776 | tf_op jit(solution)/shard_map/all_gather | solution.py:409
  295.5 2.2 copy-done
  299.7 23.8 %remap.3 = f32[256,40,128]{2,1,0:T(8,128)} custom-call(s32[1]{0:T(128)} %get-tuple-element.19.number, s32[520]{0:T(1024)S(1)} %copy-done.10, s32[520]{0:T(1024)S(1)} %copy-done.11, s32[520]{0:T(1024)S(1)} %copy-done.12, f32[512,40,128]{2,1,0:T(8,128)} %all-gather.7.cloned.1.call-done.blocks, bf16[64,128,256]{2,1,0:T(8,128)(2,1)S(1)} %copy-done), custom_call_target="tpu_custom_call" | custom-call | tf_op jit(solution)/shard_map/remap/pallas_call | solution.py:280
  323.5 41.1 %reduce-scatter.5.cloned.1.call-done.values = f32[32,40,128]{2,1,0:T(8,128)} async-done(((f32[256,40,128]{2,1,0:T(8,128)}), f32[32,40,128]{2,1,0:T(8,128)}) %reduce-scatter.5.cloned.1.call-update) | async-done | bytes 655376 | tf_op jit(solution)/shard_map/reduce_scatter | solution.py:411
  365.7 1.8 raise_levels.1
  (85 shorter events, 24.4 us)
Async XLA Ops:
  7.2 126.1 %all-gather.5.cloned.1.call-start = ((), (), s32[]{:S(2)}) async-start(), calls=%async_computation.2 | async-start | bytes 11141120 | tf_op jit(solution)/shard_map/all_gather | solution.py:397
  9.1 5.1 %collective-permute-start = (f32[200,128]{1,0:T(8,128)S(1)}, f32[200,128]{1,0:T(8,128)S(1)}, u32[]{:S(2)}, u32[]{:S(2)}) collective-permute-start(f32[200,128]{1,0:T(8,128)S(1)} %get-tuple-element.41), channel_id=1, source_target_pairs={{0,1},{1,2},{2,3},{3,4},{4,5},{5,6},{6,7},{8,9},{9,10},{10,11},{11... | collective-permute-start | bytes 307208 | tf_op jit(solution)/shard_map/ppermute | solution.py:145
  10.8 4.5 %collective-permute-start.1 = (f32[200,128]{1,0:T(8,128)S(1)}, f32[200,128]{1,0:T(8,128)S(1)}, u32[]{:S(2)}, u32[]{:S(2)}) collective-permute-start(f32[200,128]{1,0:T(8,128)S(1)} %get-tuple-element.40), channel_id=1, source_target_pairs={{1,0},{2,1},{3,2},{4,3},{5,4},{6,5},{7,6},{9,8},{10,9},{11,10},{12... | collective-permute-start | bytes 307208 | tf_op jit(solution)/shard_map/ppermute | solution.py:146
  15.3 1.1 copy-start.3
  16.4 0.7 copy-start.8
  17.8 6.3 %collective-permute-start.2 = (f32[104,128]{1,0:T(8,128)S(1)}, f32[104,128]{1,0:T(8,128)S(1)}, u32[]{:S(2)}, u32[]{:S(2)}) collective-permute-start(f32[104,128]{1,0:T(8,128)S(1)} %get-tuple-element.16), channel_id=1, source_target_pairs={{0,8},{8,16},{16,24},{24,32},{32,40},{40,48},{48,56},{56,64},{64,7... | collective-permute-start | bytes 159752 | tf_op jit(solution)/shard_map/ppermute | solution.py:158
  19.8 4.3 %collective-permute-start.3 = (f32[104,128]{1,0:T(8,128)S(1)}, f32[104,128]{1,0:T(8,128)S(1)}, u32[]{:S(2)}, u32[]{:S(2)}) collective-permute-start(f32[104,128]{1,0:T(8,128)S(1)} %get-tuple-element.17), channel_id=1, source_target_pairs={{8,0},{16,8},{24,16},{32,24},{40,32},{48,40},{56,48},{64,56},{72,6... | collective-permute-start | bytes 159752 | tf_op jit(solution)/shard_map/ppermute | solution.py:159
  24.1 1.1 copy-start.4
  25.2 0.7 copy-start.9
  47.0 154.5 %reduce-scatter.3.cloned.1.call-start = ((), (), s32[]{:S(2)}) async-start(), calls=%async_computation.3 | async-start | bytes 5898240 | tf_op jit(solution)/shard_map/reduce_scatter | solution.py:399
  83.6 2.0 copy-start.1
  133.3 2.2 copy-start.2
  136.8 0.7 copy-start.15
  160.5 0.7 copy-start.18
  160.5 0.8 copy-start.19
  160.5 1.0 copy-start.17
  160.5 1.2 copy-start.16
  160.5 41.0 %copy-start.7 = (bf16[512,512]{1,0:T(8,128)(2,1)S(1)}, bf16[512,512]{1,0:T(8,128)(2,1)}, u32[]{:S(2)}) copy-start(bf16[512,512]{1,0:T(8,128)(2,1)} %w_mid.1) | copy-start | bytes 1572868
  160.5 135.0 %all-gather.7.cloned.1.call-start = ((), (), s32[]{:S(2)}) async-start(), calls=%async_computation.4 | async-start | bytes 11141120 | tf_op jit(solution)/shard_map/all_gather | solution.py:409
  201.4 1.1 copy-start.6
  215.3 149.3 %reduce-scatter.5.cloned.1.call-start = ((), (), s32[]{:S(2)}) async-start(), calls=%async_computation.5 | async-start | bytes 5898240 | tf_op jit(solution)/shard_map/reduce_scatter | solution.py:411
  295.5 2.2 copy-start
  297.7 0.7 copy-start.10
  364.6 1.1 copy-start.5
  (4 other events, 2.7 us)
Sparse Core Ops, SparseCore 0:
  47.1 86.1 all-gather.4
  160.6 40.7 reduce-scatter.2
  215.4 80.0 all-gather.6
  323.6 40.9 reduce-scatter.4

commit v2 on v1

v2 whole, which is shorter than its diff:
```python
import functools
import math

import jax
import jax.numpy as jnp
from jax import lax
from jax.experimental import pallas as pl
from jax.experimental.pallas import tpu as pltpu
from jax.sharding import PartitionSpec as P

SWEEPS = 4
ROWS = 4
F32 = jnp.float32
BF16 = jnp.bfloat16
HIGHEST = lax.Precision.HIGHEST

VMEM_SPEC = pl.BlockSpec(memory_space=pltpu.VMEM)
HBM_SPEC = pl.BlockSpec(memory_space=pltpu.HBM)
SMEM_SPEC = pl.BlockSpec(memory_space=pltpu.SMEM)


def params(mebibytes=32):
    return pltpu.CompilerParams(vmem_limit_bytes=mebibytes * 1024 * 1024)


def cost(microseconds):
    return pl.CostEstimate(
        flops=0, transcendentals=0, bytes_accessed=int(microseconds * 3_000_000)
    )


def pack_kernel(nrows, nlev, width, state, coef, top, bottom, first_out, last_out):
    halo = SWEEPS
    lane = lax.broadcasted_iota(jnp.int32, (nlev, width), 1)
    group = lane // halo
    lane_one = lax.broadcasted_iota(jnp.int32, (1, width), 1)
    group_one = lane_one // halo

    def rows_of(e):
        if e < halo:
            return top[e * nlev : (e + 1) * nlev, :], top[halo * nlev + e : halo * nlev + e + 1, :]
        if e < halo + nrows:
            return state[e - halo], coef[e - halo : e - halo + 1, :]
        b = e - halo - nrows
        return bottom[b * nlev : (b + 1) * nlev, :], bottom[halo * nlev + b : halo * nlev + b + 1, :]

    per = width // halo
    total = nrows + 2 * halo
    tiles = -(-total // per)
    first_out[...] = jnp.zeros_like(first_out)
    last_out[...] = jnp.zeros_like(last_out)
    for tile in range(tiles):
        first = jnp.zeros((nlev, width), F32)
        last = jnp.zeros((nlev, width), F32)
        first_c = jnp.zeros((1, width), F32)
        last_c = jnp.zeros((1, width), F32)
        for i in range(min(per, total - tile * per)):
            field, number = rows_of(tile * per + i)
            at = (halo * i) % width
            up = (halo * i + halo) % width
            first = jnp.where(group == i, pltpu.roll(field, at, 1) if at else field, first)
            last = jnp.where(group == i, pltpu.roll(field, up, 1) if up else field, last)
            first_c = jnp.where(group_one == i, pltpu.roll(number, at, 1) if at else number, first_c)
            last_c = jnp.where(group_one == i, pltpu.roll(number, up, 1) if up else number, last_c)
        first_out[tile * nlev : (tile + 1) * nlev, :] = first
        last_out[tile * nlev : (tile + 1) * nlev, :] = last
        first_out[tiles * nlev + tile : tiles * nlev + tile + 1, :] = first_c
        last_out[tiles * nlev + tile : tiles * nlev + tile + 1, :] = last_c


def sweep_kernel(
    nrows, nlev, width, state, coef, top, bottom, left, right, levels, marks, field_out, source_out, a, b, c
):
    halo = SWEEPS
    per = width // halo
    total = nrows + 2 * halo
    tiles = -(-total // per)
    lane = lax.broadcasted_iota(jnp.int32, (nlev, width), 1)
    lane_one = lax.broadcasted_iota(jnp.int32, (1, width), 1)
    for e in range(total):
        if e < halo:
            field = top[e * nlev : (e + 1) * nlev, :]
            number = top[halo * nlev + e : halo * nlev + e + 1, :]
        elif e < halo + nrows:
            field = state[e - halo]
            number = coef[e - halo : e - halo + 1, :]
        else:
            r = e - halo - nrows
            field = bottom[r * nlev : (r + 1) * nlev, :]
            number = bottom[halo * nlev + r : halo * nlev + r + 1, :]
        tile, i = e // per, e % per
        to_low = (width - halo * i) % width
        to_high = (width - halo - halo * i) % width
        edges = []
        for where_, rows in ((lane, slice(tile * nlev, (tile + 1) * nlev)),
                             (lane_one, slice(tiles * nlev + tile, tiles * nlev + tile + 1))):
            r_tile = right[rows, :]
            l_tile = left[rows, :]
            r_part = pltpu.roll(r_tile, to_low, 1) if to_low else r_tile
            l_part = pltpu.roll(l_tile, to_high, 1) if to_high else l_tile
            edges.append(
                jnp.where(where_ < halo, r_part, jnp.where(where_ >= width - halo, l_part, 0.0))
            )
        a[e, :, 0:width] = field
        a[e, :, width : 2 * width] = edges[0]
        c[e, :, 0:width] = number
        c[e, :, width : 2 * width] = edges[1]

    def step(source, e):
        mid = source[e]
        beside = pltpu.roll(mid, 1, 1) + pltpu.roll(mid, 2 * width - 1, 1)
        beside = beside + source[e + 1] + source[e - 1]
        return mid + c[e] * (beside - 4.0 * mid)

    held, other = a, b
    for sweep in range(1, SWEEPS):
        low, high = sweep, total - sweep
        steps = (high - low) // ROWS

        def some(i, carry, held=held, other=other, low=low):
            done = [step(held, low + i * ROWS + r) for r in range(ROWS)]
            for r in range(ROWS):
                other[low + i * ROWS + r] = done[r]
            return carry

        lax.fori_loop(0, steps, some, 0)
        for e in range(low + steps * ROWS, high):
            other[e] = step(held, e)
        held, other = other, held

    def final(i, carry):
        done = [step(held, i * ROWS + r + halo)[:, 0:width] for r in range(ROWS)]
        for r in range(ROWS):
            field_out[i * ROWS + r] = done[r]
        for r in range(0, ROWS, 2):
            pair = jnp.concatenate([done[r], done[r + 1]], axis=1)
            lowered = jnp.dot(
                levels[...], pair, precision=HIGHEST, preferred_element_type=F32
            )
            source_out[i * ROWS + r] = lowered[:, :width]
            source_out[i * ROWS + r + 1] = lowered[:, width:]
        return carry

    lax.fori_loop(0, nrows // ROWS, final, 0)
    spare = levels.shape[0] - 1
    for b in range(marks.shape[0]):
        source_out[b, spare : spare + 1, :] = marks[b : b + 1, :]


def diffuse(state, coef, levels, marks):
    nrows, nlev, width = state.shape
    halo = SWEEPS
    per = width // halo
    total = nrows + 2 * halo
    tiles = -(-total // per)
    nx, ny = lax.axis_size("fx"), lax.axis_size("fy")
    pad = -halo % 8
    blank = jnp.zeros((pad, width), F32)

    def row_message(rows):
        return jnp.concatenate(
            [state[rows].reshape(halo * nlev, width), coef[rows], blank], axis=0
        )

    down = [(i, i + 1) for i in range(ny - 1)]
    up = [(i + 1, i) for i in range(ny - 1)]
    top = lax.ppermute(row_message(slice(nrows - halo, nrows)), "fy", down)
    bottom = lax.ppermute(row_message(slice(0, halo)), "fy", up)
    edge = jax.ShapeDtypeStruct((tiles * nlev + 8, width), F32)
    first, last = pl.pallas_call(
        functools.partial(pack_kernel, nrows, nlev, width),
        out_shape=(edge, edge),
        in_specs=[VMEM_SPEC] * 4,
        out_specs=(VMEM_SPEC, VMEM_SPEC),
        compiler_params=params(),
        cost_estimate=cost(1),
        name="pack_edges",
    )(state, coef, top, bottom)
    ahead = [(i, (i + 1) % nx) for i in range(nx)]
    behind = [((i + 1) % nx, i) for i in range(nx)]
    left = lax.ppermute(last, "fx", ahead)
    right = lax.ppermute(first, "fx", behind)
    return pl.pallas_call(
        functools.partial(sweep_kernel, nrows, nlev, width),
        out_shape=(
            jax.ShapeDtypeStruct(state.shape, F32),
            jax.ShapeDtypeStruct((nrows, levels.shape[0], width), F32),
        ),
        in_specs=[VMEM_SPEC] * 8,
        out_specs=(VMEM_SPEC, VMEM_SPEC),
        scratch_shapes=[
            pltpu.VMEM((total, nlev, 2 * width), F32),
            pltpu.VMEM((total, nlev, 2 * width), F32),
            pltpu.VMEM((total, 1, 2 * width), F32),
        ],
        compiler_params=params(),
        cost_estimate=cost(9),
        name="sweeps",
    )(state, coef, top, bottom, left, right, levels, marks)


def split(value):
    high = value.astype(BF16)
    low = (value - high.astype(F32)).astype(BF16)
    return high, low


def table_kernel(turn, table, out):
    count, rows, width = table.shape
    for k in range(count):
        weights = table[k].T if turn else table[k]
        high, low = split(weights)
        out[k, :, 0:width] = high
        out[k, :, width:] = low
    out[count] = jnp.zeros((rows, 2 * width), BF16)


def split_table(table, turn):
    count, rows, width = table.shape
    return pl.pallas_call(
        functools.partial(table_kernel, turn),
        out_shape=jax.ShapeDtypeStruct((count + 1, rows, 2 * width), BF16),
        in_specs=[VMEM_SPEC],
        out_specs=VMEM_SPEC,
        compiler_params=params(),
        cost_estimate=cost(3),
        name="split_table",
    )(table)


UNROLL = 8


PLACES = 40


def list_kernel(zero_row, values, valid, table):
    sets, room = valid.shape
    fields = values.shape[1] // room
    slot = lax.broadcasted_iota(jnp.int32, (fields * room, room), 0)
    other = lax.broadcasted_iota(jnp.int32, (fields * room, room), 1)
    within = slot % room
    transposed = (((1,), (1,)), ((), ()))

    def spread_out(chosen):
        return lax.dot_general(
            chosen.astype(F32), valid[...], transposed, preferred_element_type=F32
        )

    ahead = spread_out(other < within)
    first = lax.broadcasted_iota(jnp.int32, ahead.shape, 0) // room * PLACES + 1
    place = jnp.where(spread_out(other == within) > 0.5, ahead.astype(jnp.int32) + first, -1)
    lane = lax.broadcasted_iota(jnp.int32, (fields * room, 128), 1)
    for s in range(sets):
        chosen = (place[:, s : s + 1] == lane).astype(F32)
        table[s : s + 1, :] = jnp.dot(
            values[s : s + 1, :], chosen, preferred_element_type=F32
        )
    lane = lax.broadcasted_iota(jnp.int32, table.shape, 1)
    weight_lane = (lane > 2 * PLACES) & (lane <= 3 * PLACES)
    rows = jnp.where(weight_lane, table[...] + float(zero_row), table[...])
    number = jnp.sum(valid[...], axis=1, keepdims=True)
    table[...] = jnp.where(lane == 0, number, rows)


def slot_table(src, dst, row, count, blocks, zero_row, forward):
    sets, groups, cap = src.shape
    valid = (jnp.arange(cap, dtype=F32)[None, None, :] < count[:, :, None]).astype(F32)
    taken, given = (src, dst) if forward else (dst, src)
    given = given + blocks * jnp.arange(groups, dtype=F32)[None, :, None]
    values = jnp.stack([taken, given, row - zero_row], axis=1).reshape(sets, 3 * groups * cap)
    return pl.pallas_call(
        functools.partial(list_kernel, zero_row),
        out_shape=jax.ShapeDtypeStruct((sets, 128), F32),
        in_specs=[VMEM_SPEC] * 2,
        out_specs=VMEM_SPEC,
        cost_estimate=cost(1),
        name="slot_table",
    )(values, valid.reshape(sets, groups * cap))


def own_kernel(groups, blocks, zero_row, src, dst, row, counts, table):
    cap, owners = src.shape
    sets = table.shape[0]
    lane = lax.broadcasted_iota(jnp.int32, (owners, owners), 1)
    below = lax.broadcasted_iota(jnp.int32, (owners, owners), 0)
    same = lane // groups == below // groups
    number = counts[...].astype(F32)
    ahead = jnp.dot(number, (same & (below < lane)).astype(F32), preferred_element_type=F32)
    keys = [jnp.where(c < counts[...], ahead.astype(jnp.int32) + 1 + c, -1) for c in range(cap)]
    keys = jnp.concatenate(keys + [jnp.zeros((8 - cap, owners), jnp.int32)], axis=0).astype(F32)
    keys = keys.T.astype(jnp.int32)
    mine = lax.broadcasted_iota(jnp.int32, (sets, owners), 1) // groups == lax.broadcasted_iota(
        jnp.int32, (sets, owners), 0
    )
    which = lax.broadcasted_iota(jnp.int32, (1, owners), 1) % groups
    rows = jnp.zeros((sets, owners), F32)
    for c in range(cap):
        key = keys[:, c : c + 1]
        for f, value in enumerate(
            (src[c : c + 1, :], dst[c : c + 1, :] + which * blocks, row[c : c + 1, :] - zero_row)
        ):
            chosen = ((lane == key + f * PLACES) & (key > 0)).astype(F32)
            held = jnp.where(mine, value.astype(F32), 0.0)
            rows = rows + jnp.dot(held, chosen, preferred_element_type=F32)
    place = lax.broadcasted_iota(jnp.int32, rows.shape, 1)
    rows = jnp.where((place > 2 * PLACES) & (place <= 3 * PLACES), rows + float(zero_row), rows)
    used = jnp.sum(jnp.where(mine, number, 0.0), axis=1, keepdims=True)
    table[...] = jnp.where(place == 0, used, rows)


def own_table(src, dst, row, counts, groups, blocks, zero_row):
    owners = counts.shape[1]
    return pl.pallas_call(
        functools.partial(own_kernel, groups, blocks, zero_row),
        out_shape=jax.ShapeDtypeStruct((owners // groups, owners), F32),
        in_specs=[VMEM_SPEC] * 4,
        out_specs=VMEM_SPEC,
        cost_estimate=cost(1),
        name="own_table",
    )(src[0].T, dst[0].T, row[0].T, counts)


def remap_kernel(first, sizes, own_rows, slots, order, lines, tables, *refs):
    arrays, refs = refs[: len(sizes)], refs[len(sizes) :]
    if not first:
        start, refs = refs[0], refs[1:]
    outs, refs = (refs[:1], refs[1:]) if first else (refs[:4], refs[4:])
    blocks, weights, total, products, held_rows, scalars, sems, late_sems = refs[:8]
    features, width = total.shape[1:]
    copies, at = [], 0
    for k, size in enumerate(sizes):
        copies.append(pltpu.make_async_copy(arrays[k], blocks.at[at : at + size], sems.at[k]))
        at += size
    copies.append(pltpu.make_async_copy(tables, weights, sems.at[len(sizes)]))
    for copy in copies:
        copy.start()
    if not first:
        started = refs[8]
        fetch = pltpu.make_async_copy(start, started, late_sems.at[0])
        fetch.start()
    total[...] = jnp.zeros_like(total)
    products[...] = jnp.zeros_like(products)
    for copy in copies:
        copy.wait()
    sets = order.shape[0]
    size = blocks.shape[0] // sets
    if own_rows:
        for p in range(sets):
            held_rows[p : p + 1, :] = blocks[
                p * size + slots[0], features - 1 : features, :
            ].astype(jnp.int32)
        rows_copy = pltpu.make_async_copy(held_rows, scalars, late_sems.at[1])
        rows_copy.start()
        rows_copy.wait()
        slots = scalars

    def add(row, i):
        held = [products[u] for u in range(UNROLL)]
        for u in range(UNROLL):
            t = slots[row, 1 + PLACES + i * UNROLL + u]
            total[t] = total[t] + held[u]

    def one_set(p, carry):
        row = order[p]

        def group(i, carry):
            made = []
            for u in range(UNROLL):
                value = blocks[p * size + slots[row, 1 + i * UNROLL + u]]
                high = value.astype(BF16).astype(F32)
                both = jnp.concatenate([high, value - high], axis=0).astype(BF16)
                weight = weights[slots[row, 1 + 2 * PLACES + i * UNROLL + u]]
                r = jnp.dot(both, weight, preferred_element_type=F32)
                made.append(r[:features, :width] + r[:features, width:] + r[features:, :width])
            add(*carry)
            for u in range(UNROLL):
                products[u] = made[u]
            return row, i

        return lax.fori_loop(0, (slots[row, 0] + UNROLL - 1) // UNROLL, group, carry)

    add(*lax.fori_loop(0, sets, one_set, (order[0], 0)))
    copies = []
    if first:
        copies.append(pltpu.make_async_copy(total, outs[0], sems.at[0]))
        copies[0].start()
    else:
        fetch.wait()
        half = size // 2
        for k in range(8):
            part = slice(k * 2 * half, (k + 1) * 2 * half)
            total[part] = total[part] + started[part]
        for k, out in enumerate(outs):
            core = lines[1] if k // 2 else 1 - lines[1]
            for place, away in enumerate(AWAY):
                owner = lax.rem(lines[0] + away, 4) * 2 + core
                copies.append(
                    pltpu.make_async_copy(
                        total.at[pl.ds(owner * 2 * half + (k % 2) * half, half)],
                        out.at[place * half : (place + 1) * half],
                        sems.at[k * 4 + place],
                    )
                )
                copies[-1].start()
    for copy in copies:
        copy.wait()


AWAY = (2, 1, 3, 0)
REMAP_MIB = 32


def remap(slots, order, lines, arrays, tables, count, start):
    block = arrays[0].shape[1:]
    sizes = [a.shape[0] for a in arrays]
    first = start is None
    own_rows = slots.ndim == 1
    sets = order.shape[0]
    operands = (slots, order, lines, tables) + tuple(arrays) + (() if first else (start,))
    outs = (count,) if first else (count // 4,) * 4
    return pl.pallas_call(
        functools.partial(remap_kernel, first, sizes, own_rows),
        out_shape=[jax.ShapeDtypeStruct((n,) + block, F32) for n in outs],
        in_specs=[SMEM_SPEC] * 3 + [HBM_SPEC] * (len(operands) - 3),
        out_specs=[HBM_SPEC] * len(outs),
        scratch_shapes=[
            pltpu.VMEM((sum(sizes),) + block, F32),
            pltpu.VMEM(tables.shape, BF16),
            pltpu.VMEM((count,) + block, F32),
            pltpu.VMEM((UNROLL,) + block, F32),
            pltpu.VMEM((sets, 128), jnp.int32),
            pltpu.SMEM((sets, 128), jnp.int32),
            pltpu.SemaphoreType.DMA((16,)),
            pltpu.SemaphoreType.DMA((2,)),
        ]
        + ([] if first else [pltpu.VMEM((count,) + block, F32)]),
        compiler_params=params(REMAP_MIB),
        cost_estimate=cost(12 if first else 8),
        name="remap",
    )(*operands)


EARLY_SETS = 10


def remap_all(slots, early_order, late_order, lines, sets, tables, count):
    (start,) = remap(slots, early_order, lines, sets[0], tables, count, None)
    return remap(slots, late_order, lines, sets[1], tables, count, start)


def step(value, along, other_core=False):
    ny = lax.axis_size("fy")
    pairs = []
    for y in range(ny):
        chip, core = divmod(y, 2)
        pairs.append((y, (chip + along) % (ny // 2) * 2 + (core ^ int(other_core))))
    return lax.ppermute(value, "fy", pairs)


def gather_sums(other, mine):
    n = mine.shape[0] // 4
    h = n // 2
    got = step(other, 0, True)
    far = mine[:n] + got[:n]
    up, down = step(far[:h], 1), step(far[h:], -1)
    plus = mine[n : 2 * n] + got[n : 2 * n]
    minus = mine[2 * n : 3 * n] + got[2 * n : 3 * n]
    plus = jnp.concatenate([plus[:h] + up, plus[h:]], axis=0)
    minus = jnp.concatenate([minus[:h], minus[h:] + down], axis=0)
    return mine, got, step(plus, 1), step(minus, -1)


def hop(value, first, by):
    nx, ny = lax.axis_size("fx"), lax.axis_size("fy")
    side = math.isqrt(nx)
    pairs = []
    for x in range(nx):
        for y in range(ny):
            slow, fast = divmod(x, side)
            if first == (y % 2 == 0):
                fast = (fast + by) % side
            else:
                slow = (slow + by) % side
            pairs.append((x * ny + y, (slow * side + fast) * ny + y))
    return lax.ppermute(value, ("fx", "fy"), pairs)


def spread(own, given=(), prepare=lambda given: given):
    n = own.shape[0]
    p, m = hop(own, True, 1), hop(own, True, -1)
    bp, bm = hop(own, False, 1), hop(own, False, -1)
    p, m, bp, bm, given = lax.optimization_barrier((p, m, bp, bm, given))
    opp = hop(p, True, 1)
    pm = jnp.concatenate([p, m], axis=0)
    pmp, pmm = hop(pm, False, 1), hop(pm, False, -1)
    bo = hop(bm, False, -1)
    made = prepare(given)
    opp, pmp, pmm, bo, made = lax.optimization_barrier((opp, pmp, pmm, bo, made))
    op, om = hop(opp, False, 1), hop(opp, False, -1)
    pmo = hop(pmm, False, -1)
    oo = hop(op, False, 1)
    return ([own, p, m, bp, bm, opp, pmp, pmm], [bo, op, om, pmo, oo]), made


def spread_order(mx, my):
    side = math.isqrt(lax.axis_size("fx"))
    slow, fast = mx // side, mx % side
    turned = my % 2
    places = [(0, 0), (1, 0), (-1, 0), (0, 1), (0, -1), (2, 0), (1, 1), (-1, 1), (1, -1), (-1, -1),
              (0, 2), (2, 1), (2, -1), (1, 2), (-1, 2), (2, 2)]
    a = jnp.array([p[0] for p in places], jnp.int32)
    b = jnp.array([p[1] for p in places], jnp.int32)
    from_fast = (fast - jnp.where(turned == 0, a, b) + side) % side
    from_slow = (slow - jnp.where(turned == 0, b, a) + side) % side
    return from_slow * side + from_fast


def gelu(x):
    inner = x * (0.7978845608028654 + (0.7978845608028654 * 0.044715) * (x * x))
    half = 0.5 * x
    return half + half * jnp.tanh(inner)


def summed(parts, b):
    mine, got, plus, minus = parts
    own = 3 * plus.shape[0]
    return (mine[own + b] + got[own + b]) + (plus[b] + minus[b])


def network_kernel(at, *refs):
    parts, (w_in, b_in, w_mid, b_mid, w_out), refs = refs[:4], refs[4:9], refs[9:]
    out = refs[-1]
    width = out.shape[2]
    count = parts[2].shape[0]

    def piece(i, carry):
        pairs = [i * 4 + 2 * k for k in range(2)]
        xs = [
            jnp.concatenate([summed(parts, b), summed(parts, b + 1)], axis=1).astype(BF16)
            for b in pairs
        ]
        firsts = [jnp.dot(w_in[...], x, preferred_element_type=F32) + b_in[...] for x in xs]
        firsts = [gelu(first).astype(BF16) for first in firsts]
        seconds = [jnp.dot(w_mid[...], h, preferred_element_type=F32) + b_mid[...] for h in firsts]
        seconds = [gelu(second).astype(BF16) for second in seconds]
        for b, second in zip(pairs, seconds):
            tend = jnp.dot(w_out[...], second, preferred_element_type=F32)
            out[at + b] = tend[:, :width]
            out[at + b + 1] = tend[:, width:]
        return carry

    lax.fori_loop(0, count // 4, piece, 0)


def column_network(parts, weights, count, at, begun):
    block = parts[2].shape[1:]
    operands = tuple(parts) + tuple(weights) + (() if begun is None else (begun,))
    return pl.pallas_call(
        functools.partial(network_kernel, at),
        out_shape=jax.ShapeDtypeStruct((count,) + block, F32),
        in_specs=[VMEM_SPEC] * len(operands),
        out_specs=VMEM_SPEC,
        input_output_aliases={} if begun is None else {len(operands) - 1: 0},
        compiler_params=params(),
        cost_estimate=cost(6),
        name="column_network",
    )(*operands)


def raise_kernel(*refs):
    levels, out = refs[-2:]
    width = out.shape[2]
    at = 0
    for parts in (refs[:4], refs[4:8]):
        count = parts[2].shape[0]
        for b in range(0, count, 2):
            pair = jnp.concatenate([summed(parts, b), summed(parts, b + 1)], axis=1)
            raised = jnp.dot(levels[...], pair, precision=HIGHEST, preferred_element_type=F32)
            out[at + b] = raised[:, :width]
            out[at + b + 1] = raised[:, width:]
        at += count


def raise_levels(halves, levels):
    count = sum(parts[2].shape[0] for parts in halves)
    shape = (count, levels.shape[0], halves[0][2].shape[2])
    return pl.pallas_call(
        raise_kernel,
        out_shape=jax.ShapeDtypeStruct(shape, F32),
        in_specs=[VMEM_SPEC] * 9,
        out_specs=VMEM_SPEC,
        compiler_params=params(),
        cost_estimate=cost(2),
        name="raise_levels",
    )(*halves[0], *halves[1], levels)


def level_matrix(brackets, fractions, nlev, variables, features):
    levels = nlev // variables
    cols = jnp.arange(levels, dtype=jnp.int32)
    lower = (cols[None, :] == brackets[:, None]).astype(F32)
    upper = (cols[None, :] == brackets[:, None] + 1).astype(F32)
    one = lower * (1.0 - fractions[:, None]) + upper * fractions[:, None]
    whole = (jnp.eye(variables, dtype=F32)[:, None, :, None] * one[None, :, None, :]).reshape(
        variables * one.shape[0], nlev
    )
    return jnp.pad(whole, ((0, features - whole.shape[0]), (0, 0)))


def per_device(
    state,
    coef,
    weight_table,
    src_blocks,
    dst_blocks,
    weight_rows,
    counts,
    brackets,
    fractions,
    w_in,
    b_in,
    w_mid,
    b_mid,
    w_out,
):
    nblocks, nlev, width = state.shape
    used_features = w_in.shape[1]
    features = -(-used_features // 8) * 8
    variables = used_features // brackets.shape[0]
    nx, ny = lax.axis_size("fx"), lax.axis_size("fy")
    mx, my = lax.axis_index("fx"), lax.axis_index("fy")
    ndev, cap = src_blocks.shape[1:]

    levels = level_matrix(brackets, fractions, nlev, variables, features)
    zero_row = weight_table.shape[0]
    order = spread_order(mx, my)
    spare = features - used_features
    given = (src_blocks, dst_blocks, weight_rows, counts)
    own_rows = own_table(*given, ny, nblocks, zero_row)
    plain = split_table(weight_table, False)

    field, source = diffuse(state, coef, levels, own_rows)
    straight = jnp.arange(EARLY_SETS, dtype=jnp.int32)
    place = mx.astype(jnp.int32).reshape(1)
    lines = jnp.stack([my // 2, my % 2]).astype(jnp.int32)

    def way_back(given):
        src, dst, row, cnt, weights = given
        lists = jnp.concatenate([src[0], dst[0], row[0], cnt[0][:, None]], axis=1).astype(F32)
        one = 3 * cap + 1
        lists = lists.reshape(nx, ny, one).transpose(1, 0, 2).reshape(ny, nx * one)
        lists = lax.all_gather(lists, "fy", axis=0)
        lists = lax.dynamic_index_in_dim(lists, my, 1, False).reshape(ny, nx, one)
        lists = lists.transpose(1, 0, 2)
        table = slot_table(
            lists[..., :cap],
            lists[..., cap : 2 * cap],
            lists[..., 2 * cap : 3 * cap],
            lists[..., 3 * cap],
            nblocks,
            zero_row,
            False,
        ).astype(jnp.int32)
        return table, split_table(weights, True)

    sets, (table, turned) = spread(source, given + (weight_table,), way_back)
    sums = remap_all(
        place, straight, straight[: nx - EARLY_SETS], lines, sets, plain, ny * nblocks
    )
    network = (
        jnp.pad(w_in, ((0, 0), (0, spare))),
        b_in[:, None],
        w_mid,
        b_mid[:, None],
        jnp.pad(w_out, ((0, spare), (0, 0))),
    )
    tend, half = None, nblocks // 2
    for k in range(2):
        parts = gather_sums(sums[k], sums[2 + k])
        tend = column_network(parts, network, nblocks, k * half, tend)
    sets, _ = spread(tend)
    sums = remap_all(
        table, order[:EARLY_SETS], order[EARLY_SETS:], lines, sets, turned, ny * nblocks
    )
    halves = [gather_sums(sums[k], sums[2 + k]) for k in range(2)]
    return field, raise_levels(halves, levels.T)


def solution(mesh):
    placed = (
        P("fy", None, "fx"),
        P("fy", "fx"),
        P(),
        P(("fx", "fy"), None, None),
        P(("fx", "fy"), None, None),
        P(("fx", "fy"), None, None),
        P(("fx", "fy"), None),
        P(),
        P(),
        P(),
        P(),
        P(),
        P(),
        P(),
    )
    return jax.shard_map(
        per_device,
        mesh=mesh,
        in_specs=placed,
        out_specs=(P("fy", None, "fx"), P("fy", None, "fx")),
        check_vma=False,
    )
```

time: 375 us -> 289 us (0.77)
  waiting for transfers between devices: 176 us -> 87.3 us
  starting transfers between devices: 7.4 us -> 66 us
  Pallas kernels: 107 us -> 70.4 us
  blocking collectives: 37.2 us -> 13.1 us
  between operations: 14 us -> 1.33 us
  local copies, waits for them, and re-layouts: 29.1 us -> 41 us
  other arithmetic: 2.98 us -> 8.25 us
    all_gather x2 -> x0, waiting for transfers between devices: 92.6 us -> none  [the longest x1 53.4 us: per_device(): back = lax.all_gather(tend, 'fx', axis=0, tiled=True)]
    ppermute x0 -> x44, waiting for transfers between devices: none -> 86.2 us  [the longest x24 65.1 us: hop(): return lax.ppermute(value, ('fx', 'fy'), pairs)]
    reduce_scatter x2 -> x0, waiting for transfers between devices: 80.8 us -> none  [the longest x1 41.1 us: per_device(): returned = lax.psum_scatter(sums, 'fy', scatter_dimension=0, tiled=True)]
    ppermute x0 -> x44, starting transfers between devices: none -> 58.8 us  [the longest x24 33.7 us: hop(): return lax.ppermute(value, ('fx', 'fy'), pairs)]
    pallas_call x7 -> x11, Pallas kernels: 85.4 us -> 60.5 us  [the longest x4 42.7 us: remap(): pl.pallas_call(functools.partial(remap_kernel, first, sizes, own_rows), o...]
    all_gather x2 -> x1, blocking collectives: 37.2 us -> 13.1 us  [way_back(): lists = lax.all_gather(lists, 'fy', axis=0)]
    unnamed x42 -> x86, local copies, waits for them, and re-layouts: 17.2 us -> 30.5 us
    pallas_call x1, Pallas kernels: 21 us -> 9.22 us  [diffuse(): pl.pallas_call(functools.partial(sweep_kernel, nrows, nlev, width), out_s...]
  transfers between devices with their start and end apart: 8 -> 48, of which waited for: 6 -> 21; matrix products, arithmetic and copies ran while one was open for 4% -> 6% of each run, Pallas kernels for 6% -> 11%
where the time goes in v2:
time: 289 us; the launch traced here: 287 us
  waiting for transfers between devices  87.3 us (30%)
  Pallas kernels  70.4 us (24%)
  starting transfers between devices  66 us (23%)
  local copies, waits for them, and re-layouts  41 us (14%)
  blocking collectives  13.1 us (5%)
  other arithmetic  8.25 us (3%)
    ppermute x24, waiting for transfers between devices, hop(): return lax.ppermute(value, ('fx', 'fy'), pairs)  65.1 us
    pallas_call x4, Pallas kernels, remap(): pl.pallas_call(functools.partial(remap_kernel, first, sizes, own_rows), o...  42.7 us
    ppermute x24, starting transfers between devices, hop(): return lax.ppermute(value, ('fx', 'fy'), pairs)  33.7 us
    unnamed x86, local copies, waits for them, and re-layouts  30.5 us
    ppermute x20, starting transfers between devices, step(): return lax.ppermute(value, 'fy', pairs)  25.1 us
    ppermute x20, waiting for transfers between devices, step(): return lax.ppermute(value, 'fy', pairs)  21.1 us
    all_gather x1, blocking collectives, way_back(): lists = lax.all_gather(lists, 'fy', axis=0)  13.1 us
    pallas_call x2, Pallas kernels, column_network(): pl.pallas_call(functools.partial(network_kernel, at), out_shape=jax.Shape...  10.4 us
  transfers between devices with their start and end apart: 48, of which 21 were waited for; matrix products, arithmetic and copies ran while one was open for 6% of the time, Pallas kernels for 11%

profile of v2, /device:TPU:16, one launch (start us, length us, event | category | flops | bytes accessed | tf_op | source)
XLA Modules:
  0.0 287.4 jit_solution(178226585714364938)
XLA Ops:
  17.5 9.2 %sweeps.1 = (f32[32,48,128]{2,1,0:T(8,128)}, f32[32,40,128]{2,1,0:T(8,128)S(1)}) custom-call(f32[32,48,128]{2,1,0:T(8,128)S(1)} %copy-done.11, f32[32,128]{1,0:T(8,128)S(1)} %copy-done.30, f32[200,128]{1,0:T(8,128)S(1)} %collective-permute-done.top, f32[200,128]{1,0:T(8,128)S(1)} %collective-permute-done.1.bottom, ...), custom_call_target="tpu_custom_call" | custom-call | bytes 27000000 | tf_op jit(solution)/shard_map/sweeps/pallas_call | solution.py:183
  33.2 9.3 %collective-permute-done.4.refs_1_ = f32[32,40,128]{2,1,0:T(8,128)S(1)} collective-permute-done((f32[32,40,128]{2,1,0:T(8,128)S(1)}, f32[32,40,128]{2,1,0:T(8,128)S(1)}, u32[]{:S(2)}, u32[]{:S(2)}) %collective-permute-start.4) | collective-permute-done | bytes 655392 | tf_op jit(solution)/shard_map/ppermute | solution.py:486
  50.3 3.0 %collective-permute-start.9 = (f32[64,40,128]{2,1,0:T(8,128)}, f32[64,40,128]{2,1,0:T(8,128)}, u32[]{:S(2)}, u32[]{:S(2)}) collective-permute-start(f32[64,40,128]{2,1,0:T(8,128)} %constant_dynamic-update-slice_fusion), channel_id=1, source_target_pairs={{0,32},{1,9},{2,34},{3,11},{4,36},{5,13},{6,38},{7,15},{8,40},{9,1... | collective-permute-start | bytes 3932168 | tf_op jit(solution)/shard_map/ppermute | solution.py:486
  55.3 13.1 %all_gather.3 = f32[8,8,208]{2,1,0:T(8,128)S(1)} all-gather(f32[1,8,208]{2,1,0:T(8,128)S(1)} %all_gather_reshape.3), channel_id=1, replica_groups=mesh['fx'=16,'fy'=8] {'fy'}, dimensions={0}, use_global_device_ids=true | all-gather | bytes 59904 | tf_op jit(solution)/shard_map/all_gather | solution.py:653
  80.8 3.2 %collective-permute-start.12 = (f32[32,40,128]{2,1,0:T(8,128)}, f32[32,40,128]{2,1,0:T(8,128)}, u32[]{:S(2)}, u32[]{:S(2)}) collective-permute-start(f32[32,40,128]{2,1,0:T(8,128)} %collective-permute-done.8.refs_5_), channel_id=1, source_target_pairs={{0,32},{1,9},{2,34},{3,11},{4,36},{5,13},{6,38},{7,15},{8,40},{9,1... | collective-permute-start | bytes 1966088 | tf_op jit(solution)/shard_map/ppermute | solution.py:486
  85.9 6.5 %collective-permute-done.12.refs_1_ = f32[32,40,128]{2,1,0:T(8,128)} collective-permute-done((f32[32,40,128]{2,1,0:T(8,128)}, f32[32,40,128]{2,1,0:T(8,128)}, u32[]{:S(2)}, u32[]{:S(2)}) %collective-permute-start.12) | collective-permute-done | bytes 655392 | tf_op jit(solution)/shard_map/ppermute | solution.py:486
  103.2 11.2 %remap.4.refs_5_ = f32[256,40,128]{2,1,0:T(8,128)S(1)} custom-call(s32[1]{0:T(128)} %bitcast.17.slots, s32[10]{0:T(128)S(1)} %iota.45.order, s32[2]{0:T(128)S(1)} %pad_add_fusion.lines, bf16[65,128,256]{2,1,0:T(8,128)(2,1)S(1)} %copy-done.3, f32[32,40,128]{2,1,0:T(8,128)S(1)} %get-tuple-element.40.refs_0_, ...), custom_call_target="tpu_custom_call" | custom-call | bytes 36000000 | tf_op jit(solution)/shard_map/remap/pallas_call | solution.py:422
  114.4 10.4 %remap.5 = (f32[64,40,128]{2,1,0:T(8,128)S(1)}, f32[64,40,128]{2,1,0:T(8,128)S(1)}, f32[64,40,128]{2,1,0:T(8,128)S(1)}, f32[64,40,128]{2,1,0:T(8,128)S(1)}) custom-call(s32[1]{0:T(128)} %bitcast.17.slots, s32[6]{0:T(128)S(1)} %bitcast.38, s32[2]{0:T(128)S(1)} %pad_add_fusion.lines, bf16[65,128,256]{2,1,0:T(8,128)(2,1)S(1)} %copy-done.4, ...), custom_call_target="tpu_custom_call" | custom-call | bytes 24000000 | tf_op jit(solution)/shard_map/remap/pallas_call | solution.py:422
  139.8 3.2 %collective-permute-start.20 = (f32[16,40,128]{2,1,0:T(8,128)}, f32[16,40,128]{2,1,0:T(8,128)}, u32[]{:S(2)}, u32[]{:S(2)}) collective-permute-start(f32[16,40,128]{2,1,0:T(8,128)} %pad_maximum_fusion.1), channel_id=1, source_target_pairs={{0,6},{1,7},{2,0},{3,1},{4,2},{5,3},{6,4},{7,5},{8,14},{9,15},{10,... | collective-permute-start | bytes 983048 | tf_op jit(solution)/shard_map/ppermute | solution.py:458
  155.7 4.6 %column_network.2.refs_9_ = f32[32,40,128]{2,1,0:T(8,128)S(1)} custom-call(f32[64,40,128]{2,1,0:T(8,128)S(1)} %get-tuple-element.58.refs_0_, f32[64,40,128]{2,1,0:T(8,128)S(1)} %collective-permute-done.21.refs_1_, f32[16,40,128]{2,1,0:T(8,128)S(1)} %copy-done.28, f32[16,40,128]{2,1,0:T(8,128)S(1)} %copy-done.26, bf16[512,40]{1,0:T(8,128)(2,1)S(1)} %pad.13.refs_4_, ...), custom_call_target="tpu_custom_call" | custom-call | bytes 18000000 | tf_op jit(solution)/shard_map/column_network/pallas_call | solution.py:559
  160.4 5.7 %column_network.3.refs_0_ = f32[32,40,128]{2,1,0:T(8,128)S(1)} custom-call(f32[64,40,128]{2,1,0:T(8,128)S(1)} %copy-done.8, f32[64,40,128]{2,1,0:T(8,128)S(1)} %copy-done.10, f32[16,40,128]{2,1,0:T(8,128)} %collective-permute-done.18.refs_2_, f32[16,40,128]{2,1,0:T(8,128)} %collective-permute-done.20.refs_3_, ...), custom_call_target="tpu_custom_call", output_to_operand_aliasing={{}: (9, {})} | custom-call | bytes 18000000 | tf_op jit(solution)/shard_map/column_network/pallas_call | solution.py:559
  169.5 3.5 %collective-permute-start.28 = (f32[32,40,128]{2,1,0:T(8,128)S(1)}, f32[32,40,128]{2,1,0:T(8,128)S(1)}, u32[]{:S(2)}, u32[]{:S(2)}) collective-permute-start(f32[32,40,128]{2,1,0:T(8,128)S(1)} %column_network.3.refs_0_), channel_id=1, source_target_pairs={{0,32},{1,9},{2,34},{3,11},{4,36},{5,13},{6,38},{7,15},{8,40},{9,1... | collective-permute-start | bytes 1966088 | tf_op jit(solution)/shard_map/ppermute | solution.py:486
  173.0 11.3 %collective-permute-done.26.refs_1_ = f32[32,40,128]{2,1,0:T(8,128)S(1)} collective-permute-done((f32[32,40,128]{2,1,0:T(8,128)S(1)}, f32[32,40,128]{2,1,0:T(8,128)S(1)}, u32[]{:S(2)}, u32[]{:S(2)}) %collective-permute-start.26) | collective-permute-done | bytes 655392 | tf_op jit(solution)/shard_map/ppermute | solution.py:486
  190.1 16.8 %collective-permute-done.30.refs_5_ = f32[32,40,128]{2,1,0:T(8,128)} collective-permute-done((f32[32,40,128]{2,1,0:T(8,128)S(1)}, f32[32,40,128]{2,1,0:T(8,128)}, u32[]{:S(2)}, u32[]{:S(2)}) %collective-permute-start.30) | collective-permute-done | bytes 655392 | tf_op jit(solution)/shard_map/ppermute | solution.py:486
  207.0 5.4 %collective-permute-done.33.refs_0_ = f32[32,40,128]{2,1,0:T(8,128)S(1)} collective-permute-done((f32[32,40,128]{2,1,0:T(8,128)S(1)}, f32[32,40,128]{2,1,0:T(8,128)S(1)}, u32[]{:S(2)}, u32[]{:S(2)}) %collective-permute-start.33) | collective-permute-done | bytes 655392 | tf_op jit(solution)/shard_map/ppermute | solution.py:486
  217.1 8.4 %collective-permute-done.34.refs_1_ = f32[32,40,128]{2,1,0:T(8,128)} collective-permute-done((f32[32,40,128]{2,1,0:T(8,128)}, f32[32,40,128]{2,1,0:T(8,128)}, u32[]{:S(2)}, u32[]{:S(2)}) %collective-permute-start.34) | collective-permute-done | bytes 655392 | tf_op jit(solution)/shard_map/ppermute | solution.py:486
  233.7 11.2 %remap.6.refs_5_ = f32[256,40,128]{2,1,0:T(8,128)S(1)} custom-call(s32[16,128]{1,0:T(8,128)S(1)} %convert_element_type.29.slots, s32[10]{0:T(128)S(1)} %bitcast.37, s32[2]{0:T(128)S(1)} %pad_add_fusion.lines, bf16[65,128,256]{2,1,0:T(8,128)(2,1)S(1)} %copy-done.1, f32[32,40,128]{2,1,0:T(8,128)S(1)} %column_network.3.refs_0_, ...), custom_call_target="tpu_custom_call" | custom-call | bytes 36000000 | tf_op jit(solution)/shard_map/remap/pallas_call | solution.py:422
  245.0 10.0 %remap.7 = (f32[64,40,128]{2,1,0:T(8,128)S(1)}, f32[64,40,128]{2,1,0:T(8,128)S(1)}, f32[64,40,128]{2,1,0:T(8,128)S(1)}, f32[64,40,128]{2,1,0:T(8,128)S(1)}) custom-call(s32[16,128]{1,0:T(8,128)S(1)} %convert_element_type.29.slots, s32[6]{0:T(128)S(1)} %slice.185.order, s32[2]{0:T(128)S(1)} %pad_add_fusion.lines, bf16[65,128,256]{2,1,0:T(8,128)(2,1)S(1)} %copy-done.1, ...), custom_call_target="tpu_custom_call" | custom-call | bytes 24000000 | tf_op jit(solution)/shard_map/remap/pallas_call | solution.py:422
  261.1 3.3 %collective-permute-start.41 = (f32[8,40,128]{2,1,0:T(8,128)S(1)}, f32[8,40,128]{2,1,0:T(8,128)S(1)}, u32[]{:S(2)}, u32[]{:S(2)}) collective-permute-start(f32[8,40,128]{2,1,0:T(8,128)S(1)} %get-tuple-element.94), channel_id=1, source_target_pairs={{0,6},{1,7},{2,0},{3,1},{4,2},{5,3},{6,4},{7,5},{8,14},{9,15},{10,... | collective-permute-start | bytes 491528 | tf_op jit(solution)/shard_map/ppermute | solution.py:458
  265.4 3.7 %collective-permute-start.47 = (f32[16,40,128]{2,1,0:T(8,128)S(1)}, f32[16,40,128]{2,1,0:T(8,128)S(1)}, u32[]{:S(2)}, u32[]{:S(2)}) collective-permute-start(f32[16,40,128]{2,1,0:T(8,128)S(1)} %pad_maximum_fusion.7), channel_id=1, source_target_pairs={{0,6},{1,7},{2,0},{3,1},{4,2},{5,3},{6,4},{7,5},{8,14},{9,15},{10,... | collective-permute-start | bytes 983048 | tf_op jit(solution)/shard_map/ppermute | solution.py:458
  269.4 3.3 %collective-permute-start.42 = (f32[16,40,128]{2,1,0:T(8,128)S(1)}, f32[16,40,128]{2,1,0:T(8,128)S(1)}, u32[]{:S(2)}, u32[]{:S(2)}) collective-permute-start(f32[16,40,128]{2,1,0:T(8,128)S(1)} %pad_maximum_fusion.5), channel_id=1, source_target_pairs={{0,6},{1,7},{2,0},{3,1},{4,2},{5,3},{6,4},{7,5},{8,14},{9,15},{10,... | collective-permute-start | bytes 983048 | tf_op jit(solution)/shard_map/ppermute | solution.py:458
  272.8 4.5 %collective-permute-done.47.refs_7_ = f32[16,40,128]{2,1,0:T(8,128)S(1)} collective-permute-done((f32[16,40,128]{2,1,0:T(8,128)S(1)}, f32[16,40,128]{2,1,0:T(8,128)S(1)}, u32[]{:S(2)}, u32[]{:S(2)}) %collective-permute-start.47) | collective-permute-done | bytes 327712 | tf_op jit(solution)/shard_map/ppermute | solution.py:458
  277.3 3.8 %collective-permute-done.45.refs_6_ = f32[16,40,128]{2,1,0:T(8,128)S(1)} collective-permute-done((f32[16,40,128]{2,1,0:T(8,128)S(1)}, f32[16,40,128]{2,1,0:T(8,128)S(1)}, u32[]{:S(2)}, u32[]{:S(2)}) %collective-permute-start.45) | collective-permute-done | bytes 327712 | tf_op jit(solution)/shard_map/ppermute | solution.py:458
  282.3 3.4 %collective-permute-done.40.refs_2_ = f32[16,40,128]{2,1,0:T(8,128)S(1)} collective-permute-done((f32[16,40,128]{2,1,0:T(8,128)S(1)}, f32[16,40,128]{2,1,0:T(8,128)S(1)}, u32[]{:S(2)}, u32[]{:S(2)}) %collective-permute-start.40) | collective-permute-done | bytes 327712 | tf_op jit(solution)/shard_map/ppermute | solution.py:458
  (244 shorter events, 118.0 us)
Async XLA Ops:
  26.7 15.7 %collective-permute-start.4 = (f32[32,40,128]{2,1,0:T(8,128)S(1)}, f32[32,40,128]{2,1,0:T(8,128)S(1)}, u32[]{:S(2)}, u32[]{:S(2)}) collective-permute-start(f32[32,40,128]{2,1,0:T(8,128)S(1)} %get-tuple-element.40.refs_0_), channel_id=1, source_target_pairs={{0,8},{1,33},{2,10},{3,35},{4,12},{5,37},{6,14},{7,39},{8,16},{9,4... | collective-permute-start | bytes 1966088 | tf_op jit(solution)/shard_map/ppermute | solution.py:486
  28.2 15.5 %collective-permute-start.5 = (f32[32,40,128]{2,1,0:T(8,128)S(1)}, f32[32,40,128]{2,1,0:T(8,128)S(1)}, u32[]{:S(2)}, u32[]{:S(2)}) collective-permute-start(f32[32,40,128]{2,1,0:T(8,128)S(1)} %get-tuple-element.40.refs_0_), channel_id=1, source_target_pairs={{0,24},{1,97},{2,26},{3,99},{4,28},{5,101},{6,30},{7,103},{8,0},{9... | collective-permute-start | bytes 1966088 | tf_op jit(solution)/shard_map/ppermute | solution.py:486
  30.7 15.6 %collective-permute-start.6 = (f32[32,40,128]{2,1,0:T(8,128)S(1)}, f32[32,40,128]{2,1,0:T(8,128)S(1)}, u32[]{:S(2)}, u32[]{:S(2)}) collective-permute-start(f32[32,40,128]{2,1,0:T(8,128)S(1)} %get-tuple-element.40.refs_0_), channel_id=1, source_target_pairs={{0,32},{1,9},{2,34},{3,11},{4,36},{5,13},{6,38},{7,15},{8,40},{9,1... | collective-permute-start | bytes 1966088 | tf_op jit(solution)/shard_map/ppermute | solution.py:486
  33.2 15.3 %collective-permute-start.7 = (f32[32,40,128]{2,1,0:T(8,128)S(1)}, f32[32,40,128]{2,1,0:T(8,128)}, u32[]{:S(2)}, u32[]{:S(2)}) collective-permute-start(f32[32,40,128]{2,1,0:T(8,128)S(1)} %get-tuple-element.40.refs_0_), channel_id=1, source_target_pairs={{0,96},{1,25},{2,98},{3,27},{4,100},{5,29},{6,102},{7,31},{8,104},... | collective-permute-start | bytes 1966088 | tf_op jit(solution)/shard_map/ppermute | solution.py:486
  50.3 30.5 %collective-permute-start.10 = (f32[64,40,128]{2,1,0:T(8,128)}, f32[64,40,128]{2,1,0:T(8,128)S(1)}, u32[]{:S(2)}, u32[]{:S(2)}) collective-permute-start(f32[64,40,128]{2,1,0:T(8,128)} %constant_dynamic-update-slice_fusion), channel_id=1, source_target_pairs={{0,96},{1,25},{2,98},{3,27},{4,100},{5,29},{6,102},{7,31},{8,104},... | collective-permute-start | bytes 3932168 | tf_op jit(solution)/shard_map/ppermute | solution.py:486
  50.3 30.5 %collective-permute-start.9 = (f32[64,40,128]{2,1,0:T(8,128)}, f32[64,40,128]{2,1,0:T(8,128)}, u32[]{:S(2)}, u32[]{:S(2)}) collective-permute-start(f32[64,40,128]{2,1,0:T(8,128)} %constant_dynamic-update-slice_fusion), channel_id=1, source_target_pairs={{0,32},{1,9},{2,34},{3,11},{4,36},{5,13},{6,38},{7,15},{8,40},{9,1... | collective-permute-start | bytes 3932168 | tf_op jit(solution)/shard_map/ppermute | solution.py:486
  53.3 26.8 %collective-permute-start.8 = (f32[32,40,128]{2,1,0:T(8,128)S(1)}, f32[32,40,128]{2,1,0:T(8,128)}, u32[]{:S(2)}, u32[]{:S(2)}) collective-permute-start(f32[32,40,128]{2,1,0:T(8,128)S(1)} %collective-permute-done.4.refs_1_), channel_id=1, source_target_pairs={{0,8},{1,33},{2,10},{3,35},{4,12},{5,37},{6,14},{7,39},{8,16},{9,4... | collective-permute-start | bytes 1966088 | tf_op jit(solution)/shard_map/ppermute | solution.py:486
  84.0 30.4 %collective-permute-start.14 = (f32[64,40,128]{2,1,0:T(8,128)S(1)}, f32[64,40,128]{2,1,0:T(8,128)}, u32[]{:S(2)}, u32[]{:S(2)}) collective-permute-start(f32[64,40,128]{2,1,0:T(8,128)S(1)} %collective-permute-done.10.refs_7_), channel_id=1, source_target_pairs={{0,96},{1,25},{2,98},{3,27},{4,100},{5,29},{6,102},{7,31},{8,104},... | collective-permute-start | bytes 3932168 | tf_op jit(solution)/shard_map/ppermute | solution.py:486
  84.0 30.4 %collective-permute-start.13 = (f32[32,40,128]{2,1,0:T(8,128)}, f32[32,40,128]{2,1,0:T(8,128)}, u32[]{:S(2)}, u32[]{:S(2)}) collective-permute-start(f32[32,40,128]{2,1,0:T(8,128)} %collective-permute-done.8.refs_5_), channel_id=1, source_target_pairs={{0,96},{1,25},{2,98},{3,27},{4,100},{5,29},{6,102},{7,31},{8,104},... | collective-permute-start | bytes 1966088 | tf_op jit(solution)/shard_map/ppermute | solution.py:486
  92.4 22.0 %collective-permute-start.15 = (f32[32,40,128]{2,1,0:T(8,128)}, f32[32,40,128]{2,1,0:T(8,128)}, u32[]{:S(2)}, u32[]{:S(2)}) collective-permute-start(f32[32,40,128]{2,1,0:T(8,128)} %collective-permute-done.12.refs_1_), channel_id=1, source_target_pairs={{0,32},{1,9},{2,34},{3,11},{4,36},{5,13},{6,38},{7,15},{8,40},{9,1... | collective-permute-start | bytes 1966088 | tf_op jit(solution)/shard_map/ppermute | solution.py:486
  135.7 13.1 %collective-permute-start.25 = (f32[16,40,128]{2,1,0:T(8,128)}, f32[16,40,128]{2,1,0:T(8,128)S(1)}, u32[]{:S(2)}, u32[]{:S(2)}) collective-permute-start(f32[16,40,128]{2,1,0:T(8,128)} %pad_maximum_fusion.3), channel_id=1, source_target_pairs={{0,6},{1,7},{2,0},{3,1},{4,2},{5,3},{6,4},{7,5},{8,14},{9,15},{10,... | collective-permute-start | bytes 983048 | tf_op jit(solution)/shard_map/ppermute | solution.py:458
  139.8 20.6 %collective-permute-start.20 = (f32[16,40,128]{2,1,0:T(8,128)}, f32[16,40,128]{2,1,0:T(8,128)}, u32[]{:S(2)}, u32[]{:S(2)}) collective-permute-start(f32[16,40,128]{2,1,0:T(8,128)} %pad_maximum_fusion.1), channel_id=1, source_target_pairs={{0,6},{1,7},{2,0},{3,1},{4,2},{5,3},{6,4},{7,5},{8,14},{9,15},{10,... | collective-permute-start | bytes 983048 | tf_op jit(solution)/shard_map/ppermute | solution.py:458
  143.8 16.6 %collective-permute-start.18 = (f32[16,40,128]{2,1,0:T(8,128)}, f32[16,40,128]{2,1,0:T(8,128)}, u32[]{:S(2)}, u32[]{:S(2)}) collective-permute-start(f32[16,40,128]{2,1,0:T(8,128)} %pad_maximum_fusion), channel_id=1, source_target_pairs={{0,2},{1,3},{2,4},{3,5},{4,6},{5,7},{6,0},{7,1},{8,10},{9,11},{10,... | collective-permute-start | bytes 983048 | tf_op jit(solution)/shard_map/ppermute | solution.py:458
  166.2 18.1 %collective-permute-start.26 = (f32[32,40,128]{2,1,0:T(8,128)S(1)}, f32[32,40,128]{2,1,0:T(8,128)S(1)}, u32[]{:S(2)}, u32[]{:S(2)}) collective-permute-start(f32[32,40,128]{2,1,0:T(8,128)S(1)} %column_network.3.refs_0_), channel_id=1, source_target_pairs={{0,8},{1,33},{2,10},{3,35},{4,12},{5,37},{6,14},{7,39},{8,16},{9,4... | collective-permute-start | bytes 1966088 | tf_op jit(solution)/shard_map/ppermute | solution.py:486
  168.0 17.1 %collective-permute-start.27 = (f32[32,40,128]{2,1,0:T(8,128)S(1)}, f32[32,40,128]{2,1,0:T(8,128)S(1)}, u32[]{:S(2)}, u32[]{:S(2)}) collective-permute-start(f32[32,40,128]{2,1,0:T(8,128)S(1)} %column_network.3.refs_0_), channel_id=1, source_target_pairs={{0,24},{1,97},{2,26},{3,99},{4,28},{5,101},{6,30},{7,103},{8,0},{9... | collective-permute-start | bytes 1966088 | tf_op jit(solution)/shard_map/ppermute | solution.py:486
  169.5 15.6 %collective-permute-start.28 = (f32[32,40,128]{2,1,0:T(8,128)S(1)}, f32[32,40,128]{2,1,0:T(8,128)S(1)}, u32[]{:S(2)}, u32[]{:S(2)}) collective-permute-start(f32[32,40,128]{2,1,0:T(8,128)S(1)} %column_network.3.refs_0_), channel_id=1, source_target_pairs={{0,32},{1,9},{2,34},{3,11},{4,36},{5,13},{6,38},{7,15},{8,40},{9,1... | collective-permute-start | bytes 1966088 | tf_op jit(solution)/shard_map/ppermute | solution.py:486
  185.9 27.2 %collective-permute-start.31 = (f32[64,40,128]{2,1,0:T(8,128)S(1)}, f32[64,40,128]{2,1,0:T(8,128)S(1)}, u32[]{:S(2)}, u32[]{:S(2)}) collective-permute-start(f32[64,40,128]{2,1,0:T(8,128)S(1)} %constant_dynamic-update-slice_fusion.2), channel_id=1, source_target_pairs={{0,32},{1,9},{2,34},{3,11},{4,36},{5,13},{6,38},{7,15},{8,40},{9,1... | collective-permute-start | bytes 3932168 | tf_op jit(solution)/shard_map/ppermute | solution.py:486
  187.7 26.6 %collective-permute-start.32 = (f32[64,40,128]{2,1,0:T(8,128)S(1)}, f32[64,40,128]{2,1,0:T(8,128)S(1)}, u32[]{:S(2)}, u32[]{:S(2)}) collective-permute-start(f32[64,40,128]{2,1,0:T(8,128)S(1)} %constant_dynamic-update-slice_fusion.2), channel_id=1, source_target_pairs={{0,96},{1,25},{2,98},{3,27},{4,100},{5,29},{6,102},{7,31},{8,104},... | collective-permute-start | bytes 3932168 | tf_op jit(solution)/shard_map/ppermute | solution.py:486
  188.0 19.0 %collective-permute-start.30 = (f32[32,40,128]{2,1,0:T(8,128)S(1)}, f32[32,40,128]{2,1,0:T(8,128)}, u32[]{:S(2)}, u32[]{:S(2)}) collective-permute-start(f32[32,40,128]{2,1,0:T(8,128)S(1)} %collective-permute-done.26.refs_1_), channel_id=1, source_target_pairs={{0,8},{1,33},{2,10},{3,35},{4,12},{5,37},{6,14},{7,39},{8,16},{9,4... | collective-permute-start | bytes 1966088 | tf_op jit(solution)/shard_map/ppermute | solution.py:486
  189.5 22.9 %collective-permute-start.33 = (f32[32,40,128]{2,1,0:T(8,128)S(1)}, f32[32,40,128]{2,1,0:T(8,128)S(1)}, u32[]{:S(2)}, u32[]{:S(2)}) collective-permute-start(f32[32,40,128]{2,1,0:T(8,128)S(1)} %collective-permute-done.29.refs_4_), channel_id=1, source_target_pairs={{0,96},{1,25},{2,98},{3,27},{4,100},{5,29},{6,102},{7,31},{8,104},... | collective-permute-start | bytes 1966088 | tf_op jit(solution)/shard_map/ppermute | solution.py:486
  217.0 27.9 %collective-permute-start.36 = (f32[64,40,128]{2,1,0:T(8,128)S(1)}, f32[64,40,128]{2,1,0:T(8,128)}, u32[]{:S(2)}, u32[]{:S(2)}) collective-permute-start(f32[64,40,128]{2,1,0:T(8,128)S(1)} %collective-permute-done.32.refs_7_), channel_id=1, source_target_pairs={{0,96},{1,25},{2,98},{3,27},{4,100},{5,29},{6,102},{7,31},{8,104},... | collective-permute-start | bytes 3932168 | tf_op jit(solution)/shard_map/ppermute | solution.py:486
  217.0 27.9 %collective-permute-start.35 = (f32[32,40,128]{2,1,0:T(8,128)}, f32[32,40,128]{2,1,0:T(8,128)}, u32[]{:S(2)}, u32[]{:S(2)}) collective-permute-start(f32[32,40,128]{2,1,0:T(8,128)} %collective-permute-done.30.refs_5_), channel_id=1, source_target_pairs={{0,96},{1,25},{2,98},{3,27},{4,100},{5,29},{6,102},{7,31},{8,104},... | collective-permute-start | bytes 1966088 | tf_op jit(solution)/shard_map/ppermute | solution.py:486
  225.5 19.5 %collective-permute-start.37 = (f32[32,40,128]{2,1,0:T(8,128)}, f32[32,40,128]{2,1,0:T(8,128)}, u32[]{:S(2)}, u32[]{:S(2)}) collective-permute-start(f32[32,40,128]{2,1,0:T(8,128)} %collective-permute-done.34.refs_1_), channel_id=1, source_target_pairs={{0,32},{1,9},{2,34},{3,11},{4,36},{5,13},{6,38},{7,15},{8,40},{9,1... | collective-permute-start | bytes 1966088 | tf_op jit(solution)/shard_map/ppermute | solution.py:486
  272.7 13.0 %collective-permute-start.40 = (f32[16,40,128]{2,1,0:T(8,128)S(1)}, f32[16,40,128]{2,1,0:T(8,128)S(1)}, u32[]{:S(2)}, u32[]{:S(2)}) collective-permute-start(f32[16,40,128]{2,1,0:T(8,128)S(1)} %pad_maximum_fusion.4), channel_id=1, source_target_pairs={{0,2},{1,3},{2,4},{3,5},{4,6},{5,7},{6,0},{7,1},{8,10},{9,11},{10,... | collective-permute-start | bytes 983048 | tf_op jit(solution)/shard_map/ppermute | solution.py:458
  (65 other events, 555.3 us)

commit v3 on v2

--- a/solution.py
+++ b/solution.py
@@ -321,11 +321,13 @@
     )(src[0].T, dst[0].T, row[0].T, counts)
 
 
-def remap_kernel(first, sizes, own_rows, slots, order, lines, tables, *refs):
+def remap_kernel(first, last, marked, sizes, own_rows, slots, order, lines, tables, *refs):
     arrays, refs = refs[: len(sizes)], refs[len(sizes) :]
     if not first:
         start, refs = refs[0], refs[1:]
-    outs, refs = (refs[:1], refs[1:]) if first else (refs[:4], refs[4:])
+    if marked:
+        marks, refs = refs[0], refs[1:]
+    outs, refs = (refs[:6], refs[6:]) if last else (refs[:1], refs[1:])
     blocks, weights, total, products, held_rows, scalars, sems, late_sems = refs[:8]
     features, width = total.shape[1:]
     copies, at = [], 0
@@ -362,7 +364,7 @@
             total[t] = total[t] + held[u]
 
     def one_set(p, carry):
-        row = order[p]
+        row = p if own_rows else order[p]
 
         def group(i, carry):
             made = []
@@ -380,25 +382,36 @@
 
         return lax.fori_loop(0, (slots[row, 0] + UNROLL - 1) // UNROLL, group, carry)
 
-    add(*lax.fori_loop(0, sets, one_set, (order[0], 0)))
+    start_row = jnp.int32(0) if own_rows else order[0]
+    add(*lax.fori_loop(0, sets, one_set, (start_row, jnp.int32(0))))
+    if not first:
+        fetch.wait()
+        for k in range(8):
+            part = slice(k * size, (k + 1) * size)
+            total[part] = total[part] + started[part]
+    if marked:
+        for b in range(total.shape[0]):
+            total[b, features - 1 : features, :] = jnp.zeros((1, width), F32)
+        each = marks.shape[0] // 8
+        for k in range(8):
+            for h in range(each):
+                at = k * size + (lines[0] * 2 + lines[1]) * (size // 8) + h
+                total[at, features - 1 : features, :] = marks[k * each + h : k * each + h + 1, :]
     copies = []
-    if first:
+    if not last:
         copies.append(pltpu.make_async_copy(total, outs[0], sems.at[0]))
         copies[0].start()
     else:
-        fetch.wait()
         half = size // 2
-        for k in range(8):
-            part = slice(k * 2 * half, (k + 1) * 2 * half)
-            total[part] = total[part] + started[part]
-        for k, out in enumerate(outs):
+        for k in range(4):
             core = lines[1] if k // 2 else 1 - lines[1]
             for place, away in enumerate(AWAY):
                 owner = lax.rem(lines[0] + away, 4) * 2 + core
+                out, at = (outs[k], place) if k < 2 or place < 3 else (outs[k + 2], 0)
                 copies.append(
                     pltpu.make_async_copy(
                         total.at[pl.ds(owner * 2 * half + (k % 2) * half, half)],
-                        out.at[place * half : (place + 1) * half],
+                        out.at[at * half : (at + 1) * half],
                         sems.at[k * 4 + place],
                     )
                 )
@@ -411,18 +424,21 @@
 REMAP_MIB = 32
 
 
-def remap(slots, order, lines, arrays, tables, count, start):
+def remap(slots, order, lines, arrays, tables, count, start, last=False, marks=None):
     block = arrays[0].shape[1:]
     sizes = [a.shape[0] for a in arrays]
     first = start is None
+    marked = marks is not None
     own_rows = slots.ndim == 1
     sets = order.shape[0]
-    operands = (slots, order, lines, tables) + tuple(arrays) + (() if first else (start,))
-    outs = (count,) if first else (count // 4,) * 4
+    large = (tables,) + tuple(arrays) + (() if first else (start,))
+    small = (marks,) if marked else ()
+    quarter = count // 4
+    outs = (quarter,) * 2 + (quarter * 3 // 4,) * 2 + (quarter // 4,) * 2 if last else (count,)
     return pl.pallas_call(
-        functools.partial(remap_kernel, first, sizes, own_rows),
+        functools.partial(remap_kernel, first, last, marked, sizes, own_rows),
         out_shape=[jax.ShapeDtypeStruct((n,) + block, F32) for n in outs],
-        in_specs=[SMEM_SPEC] * 3 + [HBM_SPEC] * (len(operands) - 3),
+        in_specs=[SMEM_SPEC] * 3 + [HBM_SPEC] * len(large) + [VMEM_SPEC] * len(small),
         out_specs=[HBM_SPEC] * len(outs),
         scratch_shapes=[
             pltpu.VMEM((sum(sizes),) + block, F32),
@@ -436,17 +452,9 @@
         ]
         + ([] if first else [pltpu.VMEM((count,) + block, F32)]),
         compiler_params=params(REMAP_MIB),
-        cost_estimate=cost(12 if first else 8),
+        cost_estimate=cost(8),
         name="remap",
-    )(*operands)
-
-
-EARLY_SETS = 10
-
-
-def remap_all(slots, early_order, late_order, lines, sets, tables, count):
-    (start,) = remap(slots, early_order, lines, sets[0], tables, count, None)
-    return remap(slots, late_order, lines, sets[1], tables, count, start)
+    )(slots, order, lines, *large, *small)
 
 
 def step(value, along, other_core=False):
@@ -458,17 +466,17 @@
     return lax.ppermute(value, "fy", pairs)
 
 
-def gather_sums(other, mine):
-    n = mine.shape[0] // 4
+def gather_sums(other, mine, own):
+    n = own.shape[0]
     h = n // 2
     got = step(other, 0, True)
     far = mine[:n] + got[:n]
     up, down = step(far[:h], 1), step(far[h:], -1)
     plus = mine[n : 2 * n] + got[n : 2 * n]
-    minus = mine[2 * n : 3 * n] + got[2 * n : 3 * n]
+    minus = mine[2 * n :] + got[2 * n : 3 * n]
     plus = jnp.concatenate([plus[:h] + up, plus[h:]], axis=0)
     minus = jnp.concatenate([minus[:h], minus[h:] + down], axis=0)
-    return mine, got, step(plus, 1), step(minus, -1)
+    return own + got[3 * n :], step(plus, 1), step(minus, -1)
 
 
 def hop(value, first, by):
@@ -486,21 +494,26 @@
     return lax.ppermute(value, ("fx", "fy"), pairs)
 
 
-def spread(own, given=(), prepare=lambda given: given):
-    n = own.shape[0]
+def spread(own, given, before, weigh, count):
+    barrier = lax.optimization_barrier
+    own, given = barrier((own, given))
     p, m = hop(own, True, 1), hop(own, True, -1)
     bp, bm = hop(own, False, 1), hop(own, False, -1)
-    p, m, bp, bm, given = lax.optimization_barrier((p, m, bp, bm, given))
+    ready = before(*given)
+    p, m, bp, bm, ready = barrier((p, m, bp, bm, ready))
+    slots, order, tables, marks, other = ready
     opp = hop(p, True, 1)
     pm = jnp.concatenate([p, m], axis=0)
     pmp, pmm = hop(pm, False, 1), hop(pm, False, -1)
     bo = hop(bm, False, -1)
-    made = prepare(given)
-    opp, pmp, pmm, bo, made = lax.optimization_barrier((opp, pmp, pmm, bo, made))
+    (sums,) = weigh(slots, order[:5], [own, p, m, bp, bm], tables, None, False, None)
+    opp, pmp, pmm, bo, sums = barrier((opp, pmp, pmm, bo, sums))
     op, om = hop(opp, False, 1), hop(opp, False, -1)
     pmo = hop(pmm, False, -1)
     oo = hop(op, False, 1)
-    return ([own, p, m, bp, bm, opp, pmp, pmm], [bo, op, om, pmo, oo]), made
+    (sums,) = weigh(slots, order[5:11], [opp, pmp, pmm, bo], tables, sums, False, None)
+    marks = None if isinstance(marks, tuple) else marks
+    return weigh(slots, order[11:], [op, om, pmo, oo], tables, sums, True, marks), other
 
 
 def spread_order(mx, my):
@@ -523,23 +536,22 @@
 
 
 def summed(parts, b):
-    mine, got, plus, minus = parts
-    own = 3 * plus.shape[0]
-    return (mine[own + b] + got[own + b]) + (plus[b] + minus[b])
+    own, plus, minus = parts
+    return own[b] + (plus[b] + minus[b])
 
 
 def network_kernel(at, *refs):
-    parts, (w_in, b_in, w_mid, b_mid, w_out), refs = refs[:4], refs[4:9], refs[9:]
-    out = refs[-1]
-    width = out.shape[2]
+    parts, (w_in, b_in, w_mid, b_mid, w_out), refs = refs[:3], refs[3:8], refs[8:]
+    out, spare_rows = refs[-2:]
+    features, width = out.shape[1:]
     count = parts[2].shape[0]
 
     def piece(i, carry):
         pairs = [i * 4 + 2 * k for k in range(2)]
-        xs = [
-            jnp.concatenate([summed(parts, b), summed(parts, b + 1)], axis=1).astype(BF16)
-            for b in pairs
-        ]
+        blocks = [summed(parts, i * 4 + k) for k in range(4)]
+        for k in range(4):
+            spare_rows[pl.ds(i * 4 + k, 1), :] = blocks[k][features - 1 :]
+        xs = [jnp.concatenate(blocks[k : k + 2], axis=1).astype(BF16) for k in (0, 2)]
         firsts = [jnp.dot(w_in[...], x, preferred_element_type=F32) + b_in[...] for x in xs]
         firsts = [gelu(first).astype(BF16) for first in firsts]
         seconds = [jnp.dot(w_mid[...], h, preferred_element_type=F32) + b_mid[...] for h in firsts]
@@ -558,9 +570,12 @@
     operands = tuple(parts) + tuple(weights) + (() if begun is None else (begun,))
     return pl.pallas_call(
         functools.partial(network_kernel, at),
-        out_shape=jax.ShapeDtypeStruct((count,) + block, F32),
+        out_shape=(
+            jax.ShapeDtypeStruct((count,) + block, F32),
+            jax.ShapeDtypeStruct((parts[2].shape[0], block[1]), F32),
+        ),
         in_specs=[VMEM_SPEC] * len(operands),
-        out_specs=VMEM_SPEC,
+        out_specs=(VMEM_SPEC, VMEM_SPEC),
         input_output_aliases={} if begun is None else {len(operands) - 1: 0},
         compiler_params=params(),
         cost_estimate=cost(6),
@@ -572,7 +587,7 @@
     levels, out = refs[-2:]
     width = out.shape[2]
     at = 0
-    for parts in (refs[:4], refs[4:8]):
+    for parts in (refs[:3], refs[3:6]):
         count = parts[2].shape[0]
         for b in range(0, count, 2):
             pair = jnp.concatenate([summed(parts, b), summed(parts, b + 1)], axis=1)
@@ -588,7 +603,7 @@
     return pl.pallas_call(
         raise_kernel,
         out_shape=jax.ShapeDtypeStruct(shape, F32),
-        in_specs=[VMEM_SPEC] * 9,
+        in_specs=[VMEM_SPEC] * 7,
         out_specs=VMEM_SPEC,
         compiler_params=params(),
         cost_estimate=cost(2),
@@ -636,23 +651,32 @@
     zero_row = weight_table.shape[0]
     order = spread_order(mx, my)
     spare = features - used_features
-    given = (src_blocks, dst_blocks, weight_rows, counts)
-    own_rows = own_table(*given, ny, nblocks, zero_row)
-    plain = split_table(weight_table, False)
-
-    field, source = diffuse(state, coef, levels, own_rows)
-    straight = jnp.arange(EARLY_SETS, dtype=jnp.int32)
     place = mx.astype(jnp.int32).reshape(1)
     lines = jnp.stack([my // 2, my % 2]).astype(jnp.int32)
-
-    def way_back(given):
-        src, dst, row, cnt, weights = given
+    one = 3 * cap + 1
+    bands = ny * nblocks
+
+    def weigh(slots, order, arrays, tables, start, last, marks):
+        return remap(slots, order, lines, arrays, tables, bands, start, last, marks)
+
+    def way_out(src, dst, row, cnt, weights, w_in, b_in, w_mid, b_mid, w_out):
         lists = jnp.concatenate([src[0], dst[0], row[0], cnt[0][:, None]], axis=1).astype(F32)
-        one = 3 * cap + 1
         lists = lists.reshape(nx, ny, one).transpose(1, 0, 2).reshape(ny, nx * one)
-        lists = lax.all_gather(lists, "fy", axis=0)
-        lists = lax.dynamic_index_in_dim(lists, my, 1, False).reshape(ny, nx, one)
-        lists = lists.transpose(1, 0, 2)
+        lists = jnp.pad(lists, ((0, 0), (0, -nx * one % width))).reshape(-1, width)
+        network = (
+            jnp.pad(w_in, ((0, 0), (0, spare))),
+            b_in[:, None],
+            w_mid,
+            b_mid[:, None],
+            jnp.pad(w_out, ((0, spare), (0, 0))),
+        )
+        straight = jnp.arange(nx, dtype=jnp.int32)
+        return place, straight, split_table(weights, False), lists, network
+
+    def way_back(first, second, weights, order):
+        rows = jnp.concatenate([first, second], axis=0).reshape(ny, -1, width)
+        rows = rows[:, : -(-nx * one // width)].reshape(ny, -1)
+        lists = rows[:, : nx * one].reshape(ny, nx, one).transpose(1, 0, 2)
         table = slot_table(
             lists[..., :cap],
             lists[..., cap : 2 * cap],
@@ -661,29 +685,22 @@
             nblocks,
             zero_row,
             False,
-        ).astype(jnp.int32)
-        return table, split_table(weights, True)
-
-    sets, (table, turned) = spread(source, given + (weight_table,), way_back)
-    sums = remap_all(
-        place, straight, straight[: nx - EARLY_SETS], lines, sets, plain, ny * nblocks
-    )
-    network = (
-        jnp.pad(w_in, ((0, 0), (0, spare))),
-        b_in[:, None],
-        w_mid,
-        b_mid[:, None],
-        jnp.pad(w_out, ((0, spare), (0, 0))),
-    )
-    tend, half = None, nblocks // 2
-    for k in range(2):
-        parts = gather_sums(sums[k], sums[2 + k])
-        tend = column_network(parts, network, nblocks, k * half, tend)
-    sets, _ = spread(tend)
-    sums = remap_all(
-        table, order[:EARLY_SETS], order[EARLY_SETS:], lines, sets, turned, ny * nblocks
-    )
-    halves = [gather_sums(sums[k], sums[2 + k]) for k in range(2)]
+        )
+        return table.astype(jnp.int32), order, split_table(weights, True), (), ()
+
+    own_rows = own_table(src_blocks, dst_blocks, weight_rows, counts, ny, nblocks, zero_row)
+    field, source = diffuse(state, coef, levels, own_rows)
+    given = (src_blocks, dst_blocks, weight_rows, counts, weight_table)
+    given += (w_in, b_in, w_mid, b_mid, w_out)
+    sums, network = spread(source, given, way_out, weigh, bands)
+    half = nblocks // 2
+    parts = gather_sums(*sums[0::2])
+    tend, first = column_network(parts, network, nblocks, 0, None)
+    parts = gather_sums(*sums[1::2])
+    tend, second = column_network(parts, network, nblocks, half, tend)
+    given = (first, second, weight_table, order)
+    sums, _ = spread(tend, given, way_back, weigh, bands)
+    halves = [gather_sums(*sums[k::2]) for k in range(2)]
     return field, raise_levels(halves, levels.T)
 
 

time: 289 us -> 265 us (0.917)
  local copies, waits for them, and re-layouts: 41 us -> 26.7 us
  blocking collectives: 13.1 us -> 0 us
  starting transfers between devices: 66 us -> 59 us
  Pallas kernels: 70.4 us -> 74.7 us
  other arithmetic: 8.25 us -> 12.3 us
    all_gather x1 -> x0, blocking collectives: 13.1 us -> none  [way_back(): lists = lax.all_gather(lists, 'fy', axis=0)]
    unnamed x86 -> x75, local copies, waits for them, and re-layouts: 30.5 us -> 17.5 us
    ppermute x20, waiting for transfers between devices: 21.1 us -> 29.1 us  [step(): return lax.ppermute(value, 'fy', pairs)]
    ppermute x20, starting transfers between devices: 25.1 us -> 18.7 us  [step(): return lax.ppermute(value, 'fy', pairs)]
    ppermute x24, waiting for transfers between devices: 65.1 us -> 59.8 us  [hop(): return lax.ppermute(value, ('fx', 'fy'), pairs)]
    pallas_call x6 -> x8, Pallas kernels: 53.1 us -> 57.4 us  [the longest x6 47.3 us: remap(): pl.pallas_call(functools.partial(remap_kernel, first, last, marked, sizes...]
    add x4, other arithmetic: 0.4 us -> 3.31 us  [gather_sums(): minus = mine[2 * n:] + got[2 * n:3 * n]]
  transfers between devices with their start and end apart: 48 -> 48, of which waited for: 21 -> 25; matrix products, arithmetic and copies ran while one was open for 6% -> 7% of each run, Pallas kernels for 11% -> 15%
where the time goes in v3:
time: 265 us; the launch traced here: 264 us
  waiting for transfers between devices  90 us (34%)
  Pallas kernels  74.7 us (28%)
  starting transfers between devices  59 us (22%)
  local copies, waits for them, and re-layouts  26.7 us (10%)
  other arithmetic  12.3 us (5%)
    ppermute x24, waiting for transfers between devices, hop(): return lax.ppermute(value, ('fx', 'fy'), pairs)  59.8 us
    pallas_call x6, Pallas kernels, remap(): pl.pallas_call(functools.partial(remap_kernel, first, last, marked, sizes...  47.3 us
    ppermute x24, starting transfers between devices, hop(): return lax.ppermute(value, ('fx', 'fy'), pairs)  32.9 us
    ppermute x20, waiting for transfers between devices, step(): return lax.ppermute(value, 'fy', pairs)  29.1 us
    ppermute x20, starting transfers between devices, step(): return lax.ppermute(value, 'fy', pairs)  18.7 us
    unnamed x75, local copies, waits for them, and re-layouts  17.5 us
    pallas_call x2, Pallas kernels, column_network(): pl.pallas_call(functools.partial(network_kernel, at), out_shape=(jax.Shap...  10.1 us
    pallas_call x1, Pallas kernels, diffuse(): pl.pallas_call(functools.partial(sweep_kernel, nrows, nlev, width), out_s...  9.23 us
  transfers between devices with their start and end apart: 48, of which 25 were waited for; matrix products, arithmetic and copies ran while one was open for 7% of the time, Pallas kernels for 15%

profile of v3, /device:TPU:16, one launch (start us, length us, event | category | flops | bytes accessed | tf_op | source)
XLA Modules:
  0.0 264.1 jit_solution(16160531925970584505)
XLA Ops:
  17.7 9.2 %sweeps.1 = (f32[32,48,128]{2,1,0:T(8,128)}, f32[32,40,128]{2,1,0:T(8,128)S(1)}) custom-call(f32[32,48,128]{2,1,0:T(8,128)S(1)} %copy-done.6, f32[32,128]{1,0:T(8,128)S(1)} %copy-done.17, f32[200,128]{1,0:T(8,128)S(1)} %collective-permute-done.top, f32[200,128]{1,0:T(8,128)S(1)} %collective-permute-done.1.bottom, ...), custom_call_target="tpu_custom_call" | custom-call | bytes 27000000 | tf_op jit(solution)/shard_map/sweeps/pallas_call | solution.py:183
  50.3 3.0 %collective-permute-start.9 = (f32[64,40,128]{2,1,0:T(8,128)}, f32[64,40,128]{2,1,0:T(8,128)}, u32[]{:S(2)}, u32[]{:S(2)}) collective-permute-start(f32[64,40,128]{2,1,0:T(8,128)} %constant_dynamic-update-slice_fusion), channel_id=1, source_target_pairs={{0,32},{1,9},{2,34},{3,11},{4,36},{5,13},{6,38},{7,15},{8,40},{9,1... | collective-permute-start | bytes 3932168 | tf_op jit(solution)/shard_map/ppermute | solution.py:494
  58.9 7.0 %remap.6.refs_4_ = f32[256,40,128]{2,1,0:T(8,128)S(1)} custom-call(s32[1]{0:T(128)} %bitcast.8.slots, s32[5]{0:T(128)S(1)} %get-tuple-element.185.order, s32[2]{0:T(128)S(1)} %pad_add_fusion.lines, bf16[65,128,256]{2,1,0:T(8,128)(2,1)S(1)} %copy-done.3, f32[32,40,128]{2,1,0:T(8,128)S(1)} %copy-done.11, f32[32,40,128]{2,1,0:T(8,128)S(1)} %collective-permute-done.4.refs_1_, ...), custom_call_target="tpu_custom_call" | custom-call | bytes 24000000 | tf_op jit(solution)/shard_map/remap/pallas_call | solution.py:438
  65.9 10.1 %collective-permute-done.11.refs_3_ = f32[32,40,128]{2,1,0:T(8,128)S(1)} collective-permute-done((f32[32,40,128]{2,1,0:T(8,128)}, f32[32,40,128]{2,1,0:T(8,128)S(1)}, u32[]{:S(2)}, u32[]{:S(2)}) %collective-permute-start.11) | collective-permute-done | bytes 655392 | tf_op jit(solution)/shard_map/ppermute | solution.py:494
  76.1 3.3 %collective-permute-start.12 = (f32[32,40,128]{2,1,0:T(8,128)}, f32[32,40,128]{2,1,0:T(8,128)S(1)}, u32[]{:S(2)}, u32[]{:S(2)}) collective-permute-start(f32[32,40,128]{2,1,0:T(8,128)} %collective-permute-done.8.refs_0_), channel_id=1, source_target_pairs={{0,32},{1,9},{2,34},{3,11},{4,36},{5,13},{6,38},{7,15},{8,40},{9,1... | collective-permute-start | bytes 1966088 | tf_op jit(solution)/shard_map/ppermute | solution.py:494
  81.8 6.0 %collective-permute-done.12.refs_0_ = f32[32,40,128]{2,1,0:T(8,128)S(1)} collective-permute-done((f32[32,40,128]{2,1,0:T(8,128)}, f32[32,40,128]{2,1,0:T(8,128)S(1)}, u32[]{:S(2)}, u32[]{:S(2)}) %collective-permute-start.12) | collective-permute-done | bytes 655392 | tf_op jit(solution)/shard_map/ppermute | solution.py:494
  87.8 3.0 %collective-permute-start.15 = (f32[32,40,128]{2,1,0:T(8,128)S(1)}, f32[32,40,128]{2,1,0:T(8,128)S(1)}, u32[]{:S(2)}, u32[]{:S(2)}) collective-permute-start(f32[32,40,128]{2,1,0:T(8,128)S(1)} %collective-permute-done.12.refs_0_), channel_id=1, source_target_pairs={{0,32},{1,9},{2,34},{3,11},{4,36},{5,13},{6,38},{7,15},{8,40},{9,1... | collective-permute-start | bytes 1966088 | tf_op jit(solution)/shard_map/ppermute | solution.py:494
  90.9 7.8 %remap.7.refs_4_ = f32[256,40,128]{2,1,0:T(8,128)S(1)} custom-call(s32[1]{0:T(128)} %bitcast.8.slots, s32[6]{0:T(128)S(1)} %slice.210.order, s32[2]{0:T(128)S(1)} %pad_add_fusion.lines, bf16[65,128,256]{2,1,0:T(8,128)(2,1)S(1)} %bitcast.45, f32[32,40,128]{2,1,0:T(8,128)} %collective-permute-done.8.refs_0_, f32[64,40,128]{2,1,0:T(8,128)} %collective-permute-done.9.refs_1_, ...), custom_call_target="tpu_custom_call" | custom-call | bytes 24000000 | tf_op jit(solution)/shard_map/remap/pallas_call | solution.py:438
  98.7 6.3 %collective-permute-done.13.refs_1_ = f32[32,40,128]{2,1,0:T(8,128)S(1)} collective-permute-done((f32[32,40,128]{2,1,0:T(8,128)}, f32[32,40,128]{2,1,0:T(8,128)S(1)}, u32[]{:S(2)}, u32[]{:S(2)}) %collective-permute-start.13) | collective-permute-done | bytes 655392 | tf_op jit(solution)/shard_map/ppermute | solution.py:494
  105.0 8.9 %remap.8 = (f32[64,40,128]{2,1,0:T(8,128)}, f32[64,40,128]{2,1,0:T(8,128)}, f32[48,40,128]{2,1,0:T(8,128)S(1)}, f32[48,40,128]{2,1,0:T(8,128)S(1)}, f32[16,40,12...) custom-call(s32[1]{0:T(128)} %bitcast.8.slots, s32[5]{0:T(128)S(1)} %get-tuple-element.186.order, s32[2]{0:T(128)S(1)} %pad_add_fusion.lines, ...), custom_call_target="tpu_custom_call" | custom-call | bytes 24000000 | tf_op jit(solution)/shard_map/remap/pallas_call | solution.py:438
  138.3 3.6 %collective-permute-done.23.refs_1_ = f32[16,40,128]{2,1,0:T(8,128)S(1)} collective-permute-done((f32[16,40,128]{2,1,0:T(8,128)}, f32[16,40,128]{2,1,0:T(8,128)S(1)}, u32[]{:S(2)}, u32[]{:S(2)}) %collective-permute-start.23) | collective-permute-done | bytes 327712 | tf_op jit(solution)/shard_map/ppermute | solution.py:466
  142.0 4.6 %column_network.2 = (f32[32,40,128]{2,1,0:T(8,128)S(1)}, f32[16,128]{1,0:T(8,128)S(1)}) custom-call(f32[16,40,128]{2,1,0:T(8,128)S(1)} %get-tuple-element.148.refs_0_, f32[16,40,128]{2,1,0:T(8,128)S(1)} %collective-permute-done.23.refs_1_, f32[16,40,128]{2,1,0:T(8,128)S(1)} %collective-permute-done.25.refs_2_, bf16[512,40]{1,0:T(8,128)(2,1)S(1)} %pad.18.refs_3_, ...), custom_call_target="tpu_custom_call" | custom-call | bytes 18000000 | tf_op jit(solution)/shard_map/column_network/pallas_call | solution.py:571
  147.0 5.6 %column_network.3 = (f32[32,40,128]{2,1,0:T(8,128)S(1)}, f32[16,128]{1,0:T(8,128)S(1)}) custom-call(f32[16,40,128]{2,1,0:T(8,128)S(1)} %get-tuple-element.149.refs_0_, f32[16,40,128]{2,1,0:T(8,128)} %collective-permute-done.18.refs_1_, f32[16,40,128]{2,1,0:T(8,128)S(1)} %collective-permute-done.20.refs_2_, ...), custom_call_target="tpu_custom_call", output_to_operand_aliasing={{0}: (8, {})} | custom-call | bytes 18000000 | tf_op jit(solution)/shard_map/column_network/pallas_call | solution.py:571
  155.9 3.0 %collective-permute-start.28 = (f32[32,40,128]{2,1,0:T(8,128)S(1)}, f32[32,40,128]{2,1,0:T(8,128)S(1)}, u32[]{:S(2)}, u32[]{:S(2)}) collective-permute-start(f32[32,40,128]{2,1,0:T(8,128)S(1)} %get-tuple-element.111.refs_0_), channel_id=1, source_target_pairs={{0,32},{1,9},{2,34},{3,11},{4,36},{5,13},{6,38},{7,15},{8,40},{9,1... | collective-permute-start | bytes 1966088 | tf_op jit(solution)/shard_map/ppermute | solution.py:494
  176.9 6.8 %remap.9.refs_4_ = f32[256,40,128]{2,1,0:T(8,128)S(1)} custom-call(s32[16,128]{1,0:T(8,128)S(1)} %convert_element_type.31.slots, s32[5]{0:T(128)S(1)} %get-tuple-element.183.order, s32[2]{0:T(128)S(1)} %pad_add_fusion.lines, bf16[65,128,256]{2,1,0:T(8,128)(2,1)S(1)} %copy-done.1, f32[32,40,128]{2,1,0:T(8,128)S(1)} %get-tuple-element.111.refs_0_, ...), custom_call_target="tpu_custom_call" | custom-call | bytes 24000000 | tf_op jit(solution)/shard_map/remap/pallas_call | solution.py:438
  183.7 8.4 %collective-permute-done.30.refs_0_ = f32[32,40,128]{2,1,0:T(8,128)S(1)} collective-permute-done((f32[32,40,128]{2,1,0:T(8,128)S(1)}, f32[32,40,128]{2,1,0:T(8,128)S(1)}, u32[]{:S(2)}, u32[]{:S(2)}) %collective-permute-start.30) | collective-permute-done | bytes 655392 | tf_op jit(solution)/shard_map/ppermute | solution.py:494
  192.1 5.5 %collective-permute-done.33.refs_3_ = f32[32,40,128]{2,1,0:T(8,128)S(1)} collective-permute-done((f32[32,40,128]{2,1,0:T(8,128)S(1)}, f32[32,40,128]{2,1,0:T(8,128)S(1)}, u32[]{:S(2)}, u32[]{:S(2)}) %collective-permute-start.33) | collective-permute-done | bytes 655392 | tf_op jit(solution)/shard_map/ppermute | solution.py:494
  200.3 8.1 %collective-permute-done.34.refs_0_ = f32[32,40,128]{2,1,0:T(8,128)S(1)} collective-permute-done((f32[32,40,128]{2,1,0:T(8,128)S(1)}, f32[32,40,128]{2,1,0:T(8,128)S(1)}, u32[]{:S(2)}, u32[]{:S(2)}) %collective-permute-start.34) | collective-permute-done | bytes 655392 | tf_op jit(solution)/shard_map/ppermute | solution.py:494
  211.0 8.0 %remap.10.refs_4_ = f32[256,40,128]{2,1,0:T(8,128)S(1)} custom-call(s32[16,128]{1,0:T(8,128)S(1)} %convert_element_type.31.slots, s32[6]{0:T(128)S(1)} %slice.245.order, s32[2]{0:T(128)S(1)} %pad_add_fusion.lines, bf16[65,128,256]{2,1,0:T(8,128)(2,1)S(1)} %bitcast.43, f32[32,40,128]{2,1,0:T(8,128)S(1)} %collective-permute-done.30.refs_0_, ...), custom_call_target="tpu_custom_call" | custom-call | bytes 24000000 | tf_op jit(solution)/shard_map/remap/pallas_call | solution.py:438
  219.0 5.9 %collective-permute-done.35.refs_1_ = f32[32,40,128]{2,1,0:T(8,128)S(1)} collective-permute-done((f32[32,40,128]{2,1,0:T(8,128)S(1)}, f32[32,40,128]{2,1,0:T(8,128)S(1)}, u32[]{:S(2)}, u32[]{:S(2)}) %collective-permute-start.35) | collective-permute-done | bytes 655392 | tf_op jit(solution)/shard_map/ppermute | solution.py:494
  225.0 8.6 %remap.11 = (f32[64,40,128]{2,1,0:T(8,128)S(1)}, f32[64,40,128]{2,1,0:T(8,128)S(1)}, f32[48,40,128]{2,1,0:T(8,128)S(1)}, f32[48,40,128]{2,1,0:T(8,128)S(1)}, f32...) custom-call(s32[16,128]{1,0:T(8,128)S(1)} %convert_element_type.31.slots, s32[5]{0:T(128)S(1)} %get-tuple-element.184.order, ...), custom_call_target="tpu_custom_call" | custom-call | bytes 24000000 | tf_op jit(solution)/shard_map/remap/pallas_call | solution.py:438
  249.9 5.0 %collective-permute-done.47.refs_5_ = f32[16,40,128]{2,1,0:T(8,128)S(1)} collective-permute-done((f32[16,40,128]{2,1,0:T(8,128)S(1)}, f32[16,40,128]{2,1,0:T(8,128)S(1)}, u32[]{:S(2)}, u32[]{:S(2)}) %collective-permute-start.47) | collective-permute-done | bytes 327712 | tf_op jit(solution)/shard_map/ppermute | solution.py:466
  254.8 2.9 %collective-permute-done.45.refs_4_ = f32[16,40,128]{2,1,0:T(8,128)S(1)} collective-permute-done((f32[16,40,128]{2,1,0:T(8,128)S(1)}, f32[16,40,128]{2,1,0:T(8,128)S(1)}, u32[]{:S(2)}, u32[]{:S(2)}) %collective-permute-start.45) | collective-permute-done | bytes 327712 | tf_op jit(solution)/shard_map/ppermute | solution.py:466
  257.8 3.1 %collective-permute-done.42.refs_2_ = f32[16,40,128]{2,1,0:T(8,128)S(1)} collective-permute-done((f32[16,40,128]{2,1,0:T(8,128)S(1)}, f32[16,40,128]{2,1,0:T(8,128)S(1)}, u32[]{:S(2)}, u32[]{:S(2)}) %collective-permute-start.42) | collective-permute-done | bytes 327712 | tf_op jit(solution)/shard_map/ppermute | solution.py:466
  (241 shorter events, 119.0 us)
Async XLA Ops:
  26.9 15.7 %collective-permute-start.4 = (f32[32,40,128]{2,1,0:T(8,128)S(1)}, f32[32,40,128]{2,1,0:T(8,128)S(1)}, u32[]{:S(2)}, u32[]{:S(2)}) collective-permute-start(f32[32,40,128]{2,1,0:T(8,128)S(1)} %get-tuple-element.72.refs_0_), channel_id=1, source_target_pairs={{0,8},{1,33},{2,10},{3,35},{4,12},{5,37},{6,14},{7,39},{8,16},{9,4... | collective-permute-start | bytes 1966088 | tf_op jit(solution)/shard_map/ppermute | solution.py:494
  28.3 15.5 %collective-permute-start.5 = (f32[32,40,128]{2,1,0:T(8,128)S(1)}, f32[32,40,128]{2,1,0:T(8,128)S(1)}, u32[]{:S(2)}, u32[]{:S(2)}) collective-permute-start(f32[32,40,128]{2,1,0:T(8,128)S(1)} %get-tuple-element.72.refs_0_), channel_id=1, source_target_pairs={{0,24},{1,97},{2,26},{3,99},{4,28},{5,101},{6,30},{7,103},{8,0},{9... | collective-permute-start | bytes 1966088 | tf_op jit(solution)/shard_map/ppermute | solution.py:494
  30.7 15.7 %collective-permute-start.6 = (f32[32,40,128]{2,1,0:T(8,128)S(1)}, f32[32,40,128]{2,1,0:T(8,128)S(1)}, u32[]{:S(2)}, u32[]{:S(2)}) collective-permute-start(f32[32,40,128]{2,1,0:T(8,128)S(1)} %get-tuple-element.72.refs_0_), channel_id=1, source_target_pairs={{0,32},{1,9},{2,34},{3,11},{4,36},{5,13},{6,38},{7,15},{8,40},{9,1... | collective-permute-start | bytes 1966088 | tf_op jit(solution)/shard_map/ppermute | solution.py:494
  33.2 15.2 %collective-permute-start.7 = (f32[32,40,128]{2,1,0:T(8,128)S(1)}, f32[32,40,128]{2,1,0:T(8,128)S(1)}, u32[]{:S(2)}, u32[]{:S(2)}) collective-permute-start(f32[32,40,128]{2,1,0:T(8,128)S(1)} %get-tuple-element.72.refs_0_), channel_id=1, source_target_pairs={{0,96},{1,25},{2,98},{3,27},{4,100},{5,29},{6,102},{7,31},{8,104},... | collective-permute-start | bytes 1966088 | tf_op jit(solution)/shard_map/ppermute | solution.py:494
  50.3 25.8 %collective-permute-start.10 = (f32[64,40,128]{2,1,0:T(8,128)}, f32[64,40,128]{2,1,0:T(8,128)S(1)}, u32[]{:S(2)}, u32[]{:S(2)}) collective-permute-start(f32[64,40,128]{2,1,0:T(8,128)} %constant_dynamic-update-slice_fusion), channel_id=1, source_target_pairs={{0,96},{1,25},{2,98},{3,27},{4,100},{5,29},{6,102},{7,31},{8,104},... | collective-permute-start | bytes 3932168 | tf_op jit(solution)/shard_map/ppermute | solution.py:494
  50.3 25.8 %collective-permute-start.9 = (f32[64,40,128]{2,1,0:T(8,128)}, f32[64,40,128]{2,1,0:T(8,128)}, u32[]{:S(2)}, u32[]{:S(2)}) collective-permute-start(f32[64,40,128]{2,1,0:T(8,128)} %constant_dynamic-update-slice_fusion), channel_id=1, source_target_pairs={{0,32},{1,9},{2,34},{3,11},{4,36},{5,13},{6,38},{7,15},{8,40},{9,1... | collective-permute-start | bytes 3932168 | tf_op jit(solution)/shard_map/ppermute | solution.py:494
  53.3 22.8 %collective-permute-start.11 = (f32[32,40,128]{2,1,0:T(8,128)}, f32[32,40,128]{2,1,0:T(8,128)S(1)}, u32[]{:S(2)}, u32[]{:S(2)}) collective-permute-start(f32[32,40,128]{2,1,0:T(8,128)} %copy-done.14), channel_id=1, source_target_pairs={{0,96},{1,25},{2,98},{3,27},{4,100},{5,29},{6,102},{7,31},{8,104},... | collective-permute-start | bytes 1966088 | tf_op jit(solution)/shard_map/ppermute | solution.py:494
  53.3 22.8 %collective-permute-start.8 = (f32[32,40,128]{2,1,0:T(8,128)S(1)}, f32[32,40,128]{2,1,0:T(8,128)}, u32[]{:S(2)}, u32[]{:S(2)}) collective-permute-start(f32[32,40,128]{2,1,0:T(8,128)S(1)} %collective-permute-done.4.refs_1_), channel_id=1, source_target_pairs={{0,8},{1,33},{2,10},{3,35},{4,12},{5,37},{6,14},{7,39},{8,16},{9,4... | collective-permute-start | bytes 1966088 | tf_op jit(solution)/shard_map/ppermute | solution.py:494
  79.4 25.6 %collective-permute-start.14 = (f32[64,40,128]{2,1,0:T(8,128)S(1)}, f32[64,40,128]{2,1,0:T(8,128)S(1)}, u32[]{:S(2)}, u32[]{:S(2)}) collective-permute-start(f32[64,40,128]{2,1,0:T(8,128)S(1)} %collective-permute-done.10.refs_2_), channel_id=1, source_target_pairs={{0,96},{1,25},{2,98},{3,27},{4,100},{5,29},{6,102},{7,31},{8,104},... | collective-permute-start | bytes 3932168 | tf_op jit(solution)/shard_map/ppermute | solution.py:494
  79.4 25.6 %collective-permute-start.13 = (f32[32,40,128]{2,1,0:T(8,128)}, f32[32,40,128]{2,1,0:T(8,128)S(1)}, u32[]{:S(2)}, u32[]{:S(2)}) collective-permute-start(f32[32,40,128]{2,1,0:T(8,128)} %collective-permute-done.8.refs_0_), channel_id=1, source_target_pairs={{0,96},{1,25},{2,98},{3,27},{4,100},{5,29},{6,102},{7,31},{8,104},... | collective-permute-start | bytes 1966088 | tf_op jit(solution)/shard_map/ppermute | solution.py:494
  87.8 17.2 %collective-permute-start.15 = (f32[32,40,128]{2,1,0:T(8,128)S(1)}, f32[32,40,128]{2,1,0:T(8,128)S(1)}, u32[]{:S(2)}, u32[]{:S(2)}) collective-permute-start(f32[32,40,128]{2,1,0:T(8,128)S(1)} %collective-permute-done.12.refs_0_), channel_id=1, source_target_pairs={{0,32},{1,9},{2,34},{3,11},{4,36},{5,13},{6,38},{7,15},{8,40},{9,1... | collective-permute-start | bytes 1966088 | tf_op jit(solution)/shard_map/ppermute | solution.py:494
  131.1 15.4 %collective-permute-start.20 = (f32[16,40,128]{2,1,0:T(8,128)}, f32[16,40,128]{2,1,0:T(8,128)S(1)}, u32[]{:S(2)}, u32[]{:S(2)}) collective-permute-start(f32[16,40,128]{2,1,0:T(8,128)} %pad_maximum_fusion.1), channel_id=1, source_target_pairs={{0,6},{1,7},{2,0},{3,1},{4,2},{5,3},{6,4},{7,5},{8,14},{9,15},{10,... | collective-permute-start | bytes 983048 | tf_op jit(solution)/shard_map/ppermute | solution.py:466
  152.6 18.4 %collective-permute-start.26 = (f32[32,40,128]{2,1,0:T(8,128)S(1)}, f32[32,40,128]{2,1,0:T(8,128)S(1)}, u32[]{:S(2)}, u32[]{:S(2)}) collective-permute-start(f32[32,40,128]{2,1,0:T(8,128)S(1)} %get-tuple-element.111.refs_0_), channel_id=1, source_target_pairs={{0,8},{1,33},{2,10},{3,35},{4,12},{5,37},{6,14},{7,39},{8,16},{9,4... | collective-permute-start | bytes 1966088 | tf_op jit(solution)/shard_map/ppermute | solution.py:494
  153.3 17.7 %collective-permute-start.27 = (f32[32,40,128]{2,1,0:T(8,128)S(1)}, f32[32,40,128]{2,1,0:T(8,128)S(1)}, u32[]{:S(2)}, u32[]{:S(2)}) collective-permute-start(f32[32,40,128]{2,1,0:T(8,128)S(1)} %get-tuple-element.111.refs_0_), channel_id=1, source_target_pairs={{0,24},{1,97},{2,26},{3,99},{4,28},{5,101},{6,30},{7,103},{8,0},{9... | collective-permute-start | bytes 1966088 | tf_op jit(solution)/shard_map/ppermute | solution.py:494
  155.9 15.1 %collective-permute-start.28 = (f32[32,40,128]{2,1,0:T(8,128)S(1)}, f32[32,40,128]{2,1,0:T(8,128)S(1)}, u32[]{:S(2)}, u32[]{:S(2)}) collective-permute-start(f32[32,40,128]{2,1,0:T(8,128)S(1)} %get-tuple-element.111.refs_0_), channel_id=1, source_target_pairs={{0,32},{1,9},{2,34},{3,11},{4,36},{5,13},{6,38},{7,15},{8,40},{9,1... | collective-permute-start | bytes 1966088 | tf_op jit(solution)/shard_map/ppermute | solution.py:494
  171.2 26.4 %collective-permute-start.31 = (f32[64,40,128]{2,1,0:T(8,128)S(1)}, f32[64,40,128]{2,1,0:T(8,128)S(1)}, u32[]{:S(2)}, u32[]{:S(2)}) collective-permute-start(f32[64,40,128]{2,1,0:T(8,128)S(1)} %constant_dynamic-update-slice_fusion.2), channel_id=1, source_target_pairs={{0,32},{1,9},{2,34},{3,11},{4,36},{5,13},{6,38},{7,15},{8,40},{9,1... | collective-permute-start | bytes 3932168 | tf_op jit(solution)/shard_map/ppermute | solution.py:494
  173.0 24.6 %collective-permute-start.32 = (f32[64,40,128]{2,1,0:T(8,128)S(1)}, f32[64,40,128]{2,1,0:T(8,128)S(1)}, u32[]{:S(2)}, u32[]{:S(2)}) collective-permute-start(f32[64,40,128]{2,1,0:T(8,128)S(1)} %constant_dynamic-update-slice_fusion.2), channel_id=1, source_target_pairs={{0,96},{1,25},{2,98},{3,27},{4,100},{5,29},{6,102},{7,31},{8,104},... | collective-permute-start | bytes 3932168 | tf_op jit(solution)/shard_map/ppermute | solution.py:494
  173.2 18.9 %collective-permute-start.30 = (f32[32,40,128]{2,1,0:T(8,128)S(1)}, f32[32,40,128]{2,1,0:T(8,128)S(1)}, u32[]{:S(2)}, u32[]{:S(2)}) collective-permute-start(f32[32,40,128]{2,1,0:T(8,128)S(1)} %collective-permute-done.26.refs_1_), channel_id=1, source_target_pairs={{0,8},{1,33},{2,10},{3,35},{4,12},{5,37},{6,14},{7,39},{8,16},{9,4... | collective-permute-start | bytes 1966088 | tf_op jit(solution)/shard_map/ppermute | solution.py:494
  174.1 23.5 %collective-permute-start.33 = (f32[32,40,128]{2,1,0:T(8,128)S(1)}, f32[32,40,128]{2,1,0:T(8,128)S(1)}, u32[]{:S(2)}, u32[]{:S(2)}) collective-permute-start(f32[32,40,128]{2,1,0:T(8,128)S(1)} %collective-permute-done.29.refs_4_), channel_id=1, source_target_pairs={{0,96},{1,25},{2,98},{3,27},{4,100},{5,29},{6,102},{7,31},{8,104},... | collective-permute-start | bytes 1966088 | tf_op jit(solution)/shard_map/ppermute | solution.py:494
  200.3 24.6 %collective-permute-start.36 = (f32[64,40,128]{2,1,0:T(8,128)S(1)}, f32[64,40,128]{2,1,0:T(8,128)S(1)}, u32[]{:S(2)}, u32[]{:S(2)}) collective-permute-start(f32[64,40,128]{2,1,0:T(8,128)S(1)} %collective-permute-done.32.refs_2_), channel_id=1, source_target_pairs={{0,96},{1,25},{2,98},{3,27},{4,100},{5,29},{6,102},{7,31},{8,104},... | collective-permute-start | bytes 3932168 | tf_op jit(solution)/shard_map/ppermute | solution.py:494
  200.3 24.6 %collective-permute-start.35 = (f32[32,40,128]{2,1,0:T(8,128)S(1)}, f32[32,40,128]{2,1,0:T(8,128)S(1)}, u32[]{:S(2)}, u32[]{:S(2)}) collective-permute-start(f32[32,40,128]{2,1,0:T(8,128)S(1)} %collective-permute-done.30.refs_0_), channel_id=1, source_target_pairs={{0,96},{1,25},{2,98},{3,27},{4,100},{5,29},{6,102},{7,31},{8,104},... | collective-permute-start | bytes 1966088 | tf_op jit(solution)/shard_map/ppermute | solution.py:494
  208.4 16.5 %collective-permute-start.37 = (f32[32,40,128]{2,1,0:T(8,128)S(1)}, f32[32,40,128]{2,1,0:T(8,128)S(1)}, u32[]{:S(2)}, u32[]{:S(2)}) collective-permute-start(f32[32,40,128]{2,1,0:T(8,128)S(1)} %collective-permute-done.34.refs_0_), channel_id=1, source_target_pairs={{0,32},{1,9},{2,34},{3,11},{4,36},{5,13},{6,38},{7,15},{8,40},{9,1... | collective-permute-start | bytes 1966088 | tf_op jit(solution)/shard_map/ppermute | solution.py:494
  247.6 13.2 %collective-permute-start.42 = (f32[16,40,128]{2,1,0:T(8,128)S(1)}, f32[16,40,128]{2,1,0:T(8,128)S(1)}, u32[]{:S(2)}, u32[]{:S(2)}) collective-permute-start(f32[16,40,128]{2,1,0:T(8,128)S(1)} %pad_maximum_fusion.5), channel_id=1, source_target_pairs={{0,6},{1,7},{2,0},{3,1},{4,2},{5,3},{6,4},{7,5},{8,14},{9,15},{10,... | collective-permute-start | bytes 983048 | tf_op jit(solution)/shard_map/ppermute | solution.py:466
  249.3 13.1 %collective-permute-start.40 = (f32[16,40,128]{2,1,0:T(8,128)S(1)}, f32[16,40,128]{2,1,0:T(8,128)S(1)}, u32[]{:S(2)}, u32[]{:S(2)}) collective-permute-start(f32[16,40,128]{2,1,0:T(8,128)S(1)} %pad_maximum_fusion.4), channel_id=1, source_target_pairs={{0,2},{1,3},{2,4},{3,5},{4,6},{5,7},{6,0},{7,1},{8,10},{9,11},{10,... | collective-permute-start | bytes 983048 | tf_op jit(solution)/shard_map/ppermute | solution.py:466
  (59 other events, 597.4 us)
